TPU v7x, 32 devices: a whole 2x2x4 slice. The times are simulated.
32 devices in a mesh: pts: 32 (over z, y, x, core).
Axes of the slice: x: 2, y: 2, z: 4, core: 2. Of those that a mesh axis runs over, the one named last changes fastest.
Arguments:
- features: bfloat16 [131072, 256], P('pts'), may hold values from -6 to 6
- coords: float32 [2, 131072], P(None, 'pts'), may hold values from 0 to 1
- fourier_basis: float32 [2, 64], replicated, may hold values from -4 to 4
- block_items: int32 [1024], P('pts'), may hold values from 0 to 15, as said below
- point_mask: int32 [131072], P('pts'), may hold values from 0 to 1, as said below
- cotangent: bfloat16 [131072, 256], P('pts'), may hold values from -6 to 6
- square_weight: float32 [7, 65536], P(None, 'pts')
- square_first: float32 [7, 65536], P(None, 'pts'), may hold values from -0.00061035156 to 0.00061035156
- square_second: float32 [7, 65536], P(None, 'pts'), may hold values from 2.5518217e-08 to 4.1221733e-07
- expand_weight: float32 [2, 131072], P(None, 'pts'), may hold values from -0.375 to 0.375
- expand_first: float32 [2, 131072], P(None, 'pts'), may hold values from -0.00061035156 to 0.00061035156
- expand_second: float32 [2, 131072], P(None, 'pts'), may hold values from 2.5518217e-08 to 4.1221733e-07
- contract_weight: float32 [2, 131072], P(None, 'pts'), may hold values from -0.25 to 0.25
- contract_first: float32 [2, 131072], P(None, 'pts'), may hold values from -0.00061035156 to 0.00061035156
- contract_second: float32 [2, 131072], P(None, 'pts'), may hold values from 2.5518217e-08 to 4.1221733e-07
- fourier_weight: float32 [32768], P('pts'), may hold values from -0.5 to 0.5
- fourier_first: float32 [32768], P('pts'), may hold values from -0.00061035156 to 0.00061035156
- fourier_second: float32 [32768], P('pts'), may hold values from 2.5518217e-08 to 4.1221733e-07
- vector_weight: float32 [8, 256], replicated
- vector_first: float32 [8, 256], replicated, may hold values from -0.001953125 to 0.001953125
- vector_second: float32 [8, 256], replicated, may hold values from 2.3555276e-07 to 3.7295854e-06
- hidden_weight: float32 [2, 512], replicated, may hold values from -1.8 to 1.8
- hidden_first: float32 [2, 512], replicated, may hold values from -0.001953125 to 0.001953125
- hidden_second: float32 [2, 512], replicated, may hold values from 7.361024e-09 to 1.1777638e-07
Outputs:
- layer_output: bfloat16 [131072, 256], P('pts')
- input_grad: float32 [131072, 256], P('pts')
- grad_norm: float32 [], replicated
- new_square_first: float32 [7, 65536], P(None, 'pts')
- new_square_second: float32 [7, 65536], P(None, 'pts')
- new_square_weight: float32 [7, 65536], P(None, 'pts')
- new_expand_first: float32 [2, 131072], P(None, 'pts')
- new_expand_second: float32 [2, 131072], P(None, 'pts')
- new_expand_weight: float32 [2, 131072], P(None, 'pts')
- new_contract_first: float32 [2, 131072], P(None, 'pts')
- new_contract_second: float32 [2, 131072], P(None, 'pts')
- new_contract_weight: float32 [2, 131072], P(None, 'pts')
- new_fourier_first: float32 [32768], P('pts')
- new_fourier_second: float32 [32768], P('pts')
- new_fourier_weight: float32 [32768], P('pts')
- new_vector_first: float32 [8, 256], replicated
- new_vector_second: float32 [8, 256], replicated
- new_vector_weight: float32 [8, 256], replicated
- new_hidden_first: float32 [2, 512], replicated
- new_hidden_second: float32 [2, 512], replicated
- new_hidden_weight: float32 [2, 512], replicated
Inputs may be any that keep to these rules, and one draw needn't show every extreme that they name: `block_items`: each of the 16 items owns two or more blocks of 128 points; the item of the first block also owns the last block. `point_mask`: the first point of every block of 128 points is 1.
All inputs are finite; a program needn't handle non-finite values.
Results may differ from a plain program's by a relative error of at most 0.02.
Values may be sent and summed in bfloat16 or wider, within the bound.
A program may use at most 192 MiB of HBM per device.

v0:
```python
import math

import jax
import jax.numpy as jnp
from jax import lax
from jax.sharding import PartitionSpec as P

H = 8
E = 32
F = 512
FOUR = 128
BLOCK = 128
ITEM_PTS = 8192
STEP = 10


NORM_EPS = 1e-05
GELU_C = math.sqrt(2.0 / math.pi)
GELU_A = 0.044715
BETA_ONE = 0.9
BETA_TWO = 0.95
ADAM_EPS = 1e-08
WEIGHT_DECAY = 0.1
RATE_MATRIX = 0.05
RATE_VECTOR = 0.25
CLIP_NORM = 1.0
HIGHEST_PRECISION = lax.Precision.HIGHEST


def matmul(left, right):
    return jnp.dot(left, right, preferred_element_type=jnp.float32)


def matmul_left(left, right):
    return lax.dot_general(
        left, right, (((0,), (0,)), ((), ())), preferred_element_type=jnp.float32
    )


def matmul_right(left, right):
    return lax.dot_general(
        left, right, (((1,), (1,)), ((), ())), preferred_element_type=jnp.float32
    )


def gelu(values):
    return 0.5 * values * (1.0 + jnp.tanh(GELU_C * (values + GELU_A * values * values * values)))


def gelu_slope(values):
    tangent = jnp.tanh(GELU_C * (values + GELU_A * values * values * values))
    return 0.5 * (1.0 + tangent) + 0.5 * values * (1.0 - tangent * tangent) * GELU_C * (
        1.0 + 3.0 * GELU_A * values * values
    )


def norm_parts(values, norm_gain, norm_bias):
    centred = values - jnp.mean(values, axis=-1, keepdims=True)
    variance = jnp.mean(centred * centred, axis=-1, keepdims=True)
    root_inv = lax.rsqrt(variance + NORM_EPS)
    scaled = centred * root_inv
    return (scaled * norm_gain + norm_bias, scaled, root_inv)


def norm_back(upstream, scaled, root_inv, norm_gain):
    through = upstream * norm_gain
    centre = jnp.mean(through, axis=-1, keepdims=True)
    along = jnp.mean(through * scaled, axis=-1, keepdims=True)
    return root_inv * (through - centre - scaled * along)


def rotary_tables(coords):
    quarter = E // 4
    frequency = math.pi * (jnp.arange(quarter, dtype=jnp.float32) + 1.0) / quarter
    first_angle = coords[0][:, None] * frequency[None, :]
    second_angle = coords[1][:, None] * frequency[None, :]
    angles = jnp.concatenate([first_angle, first_angle, second_angle, second_angle], axis=1)
    return (jnp.cos(angles), jnp.sin(angles))


def rotate(values, cosine, sine):
    quarter = E // 4
    swapped = jnp.concatenate(
        [
            -values[..., quarter : 2 * quarter],
            values[..., :quarter],
            -values[..., 3 * quarter :],
            values[..., 2 * quarter : 3 * quarter],
        ],
        axis=-1,
    )
    return values * cosine[:, None, :] + swapped * sine[:, None, :]


def rotate_back(grads, cosine, sine):
    quarter = E // 4
    scaled = grads * sine[:, None, :]
    swapped = jnp.concatenate(
        [
            scaled[..., quarter : 2 * quarter],
            -scaled[..., :quarter],
            scaled[..., 3 * quarter :],
            -scaled[..., 2 * quarter : 3 * quarter],
        ],
        axis=-1,
    )
    return grads * cosine[:, None, :] + swapped


def fourier_features(coords, fourier_basis):
    phases = (
        2.0
        * math.pi
        * (
            coords[0][:, None] * fourier_basis[0][None, :]
            + coords[1][:, None] * fourier_basis[1][None, :]
        )
    )
    return jnp.concatenate([jnp.cos(phases), jnp.sin(phases)], axis=1)


def block_table(left, right, onehot):
    blocks = onehot.shape[0]
    per_block = jnp.einsum(
        "bphe,bphf->bhef",
        left.reshape(blocks, BLOCK, H, E),
        right.reshape(blocks, BLOCK, H, E),
        preferred_element_type=jnp.float32,
    )
    return jnp.einsum("ba,bhef->ahef", onehot, per_block, precision=HIGHEST_PRECISION)


def scale_round(table, inverse_count):
    return (table * inverse_count[:, None, None, None]).astype(jnp.bfloat16)


def spread(summary, onehot):
    selected = jnp.einsum(
        "ba,ahef->bhef", onehot.astype(jnp.bfloat16), summary, preferred_element_type=jnp.float32
    )
    return selected.astype(jnp.bfloat16)


def apply_summary(rows_low, block_summary, transposed):
    blocks = block_summary.shape[0]
    pattern = "bphf,bhef->bphe" if transposed else "bphe,bhef->bphf"
    mixed = jnp.einsum(
        pattern,
        rows_low.reshape(blocks, BLOCK, H, E),
        block_summary,
        preferred_element_type=jnp.float32,
    )
    return mixed.reshape(-1, H * E)


def galerkin_backward(
    grad_low, queries_low, keys_masked, values_low, block_summary, onehot, mask_float, reducer
):
    grad_masked = grad_low * mask_float.astype(jnp.bfloat16)
    grad_queries = apply_summary(grad_masked, block_summary, True)
    summary_grad = reducer(block_table(queries_low, grad_masked, onehot))
    block_grad = spread(summary_grad, onehot)
    grad_keys = apply_summary(values_low, block_grad, True) * mask_float
    grad_values = apply_summary(keys_masked, block_grad, False)
    return (grad_queries, grad_keys, grad_values)


def adam_update(weight, first, second, grad, factor, rate):
    clipped = grad * factor
    new_first = BETA_ONE * first + (1.0 - BETA_ONE) * clipped
    new_second = BETA_TWO * second + (1.0 - BETA_TWO) * clipped * clipped
    first_hat = new_first / (1.0 - BETA_ONE**STEP)
    second_hat = new_second / (1.0 - BETA_TWO**STEP)
    new_weight = weight - rate * (
        first_hat / (jnp.sqrt(second_hat) + ADAM_EPS) + WEIGHT_DECAY * weight
    )
    return (new_first, new_second, new_weight)


def own_share(full, width, along, start_index):
    return lax.dynamic_slice_in_dim(full, start_index * width, width, along)


def shards(
    features,
    coords,
    fourier_basis,
    block_items,
    point_mask,
    cotangent,
    square_weight,
    square_first,
    square_second,
    expand_weight,
    expand_first,
    expand_second,
    contract_weight,
    contract_first,
    contract_second,
    fourier_weight,
    fourier_first,
    fourier_second,
    vector_weight,
    vector_first,
    vector_second,
    hidden_weight,
    hidden_first,
    hidden_second,
):
    rows = features.shape[0]
    width = features.shape[1]
    blocks = rows // BLOCK
    devices = lax.axis_size("pts")
    items_total = rows * devices // ITEM_PTS
    gathered = (
        lax.all_gather(square_weight.astype(jnp.bfloat16), "pts", axis=1, tiled=True),
        lax.all_gather(expand_weight.astype(jnp.bfloat16), "pts", axis=1, tiled=True),
        lax.all_gather(contract_weight.astype(jnp.bfloat16), "pts", axis=1, tiled=True),
        lax.all_gather(fourier_weight.astype(jnp.bfloat16), "pts", axis=0, tiled=True),
    )
    square_full = gathered[0].reshape(7, width, width)
    expand_full = gathered[1].reshape(2, width, F)
    contract_full = gathered[2].reshape(2, F, width)
    fourier_full = gathered[3].reshape(FOUR, width)
    onehot = (block_items[:, None] == jnp.arange(items_total, dtype=jnp.int32)[None, :]).astype(
        jnp.float32
    )
    mask_float = point_mask.astype(jnp.float32)[:, None]
    mask_low = mask_float.astype(jnp.bfloat16)
    block_count = jnp.sum(mask_float.reshape(blocks, BLOCK), axis=1)
    local_count = jnp.dot(block_count, onehot, precision=HIGHEST_PRECISION)
    cosine, sine = rotary_tables(coords)
    phase_low = fourier_features(coords, fourier_basis).astype(jnp.bfloat16)
    inputs = features.astype(jnp.float32)
    normed, scaled_one, root_one = norm_parts(inputs, vector_weight[0], vector_weight[1])
    normed_low = normed.astype(jnp.bfloat16)
    joint_weight = jnp.concatenate([square_full[0], square_full[1], square_full[2]], axis=1)
    projected = matmul(normed_low, joint_weight)
    queries_low = (
        rotate(projected[:, :width].reshape(rows, H, E), cosine, sine)
        .reshape(rows, width)
        .astype(jnp.bfloat16)
    )
    keys_low = (
        rotate(projected[:, width : 2 * width].reshape(rows, H, E), cosine, sine)
        .reshape(rows, width)
        .astype(jnp.bfloat16)
    )
    keys_masked = keys_low * mask_low
    values_low = projected[:, 2 * width :].astype(jnp.bfloat16)
    self_local = block_table(keys_masked, values_low, onehot)
    self_table, item_count = lax.psum((self_local, local_count), "pts")
    inverse_count = 1.0 / item_count
    self_items = scale_round(self_table, inverse_count)
    self_summary = spread(self_items, onehot)
    attended_low = (apply_summary(queries_low, self_summary, False) * mask_float).astype(
        jnp.bfloat16
    )
    first_sum = inputs + matmul(attended_low, square_full[3])
    normed_mid, scaled_two, root_two = norm_parts(first_sum, vector_weight[2], vector_weight[3])
    middle_low = normed_mid.astype(jnp.bfloat16)
    hidden_pre = matmul(middle_low, expand_full[0]) + hidden_weight[0]
    hidden_low = gelu(hidden_pre).astype(jnp.bfloat16)
    encoded = first_sum + matmul(hidden_low, contract_full[0]) + vector_weight[6]
    normed_out, scaled_three, root_three = norm_parts(encoded, vector_weight[4], vector_weight[5])
    outer_low = normed_out.astype(jnp.bfloat16)
    pair_weight = jnp.concatenate([square_full[4], square_full[5]], axis=1)
    cross_projected = matmul(outer_low, pair_weight)
    cross_keys = cross_projected[:, :width].astype(jnp.bfloat16) * mask_low
    cross_values = cross_projected[:, width:].astype(jnp.bfloat16)
    cross_queries = matmul(phase_low, fourier_full).astype(jnp.bfloat16)
    cross_local = block_table(cross_keys, cross_values, onehot)
    cross_items = scale_round(lax.psum(cross_local, "pts"), inverse_count)
    cross_summary = spread(cross_items, onehot)
    decoded_low = (apply_summary(cross_queries, cross_summary, False) * mask_float).astype(
        jnp.bfloat16
    )
    latent = matmul(decoded_low, square_full[6])
    latent_low = latent.astype(jnp.bfloat16)
    spread_pre = matmul(latent_low, expand_full[1]) + hidden_weight[1]
    spread_low = gelu(spread_pre).astype(jnp.bfloat16)
    output = latent + matmul(spread_low, contract_full[1]) + vector_weight[7]
    cross_reducer = lambda table_part: scale_round(lax.psum(table_part, "pts"), inverse_count)
    self_reducer = lambda table_part: scale_round(lax.psum(table_part, "pts"), inverse_count)
    grad_output = cotangent.astype(jnp.float32)
    grad_bias_end = jnp.sum(grad_output, axis=0)
    grad_contract_spread = matmul_left(spread_low, cotangent)
    grad_spread = matmul_right(cotangent, contract_full[1]) * gelu_slope(spread_pre)
    grad_hidden_spread = jnp.sum(grad_spread, axis=0)
    grad_spread_low = grad_spread.astype(jnp.bfloat16)
    grad_expand_spread = matmul_left(latent_low, grad_spread_low)
    grad_latent = (grad_output + matmul_right(grad_spread_low, expand_full[1])).astype(jnp.bfloat16)
    grad_out_cross = matmul_left(decoded_low, grad_latent)
    grad_decoded = matmul_right(grad_latent, square_full[6]).astype(jnp.bfloat16)
    cross_back = galerkin_backward(
        grad_decoded,
        cross_queries,
        cross_keys,
        cross_values,
        cross_summary,
        onehot,
        mask_float,
        cross_reducer,
    )
    grad_fourier_full = matmul_left(phase_low, cross_back[0].astype(jnp.bfloat16))
    grad_pair_low = jnp.concatenate([cross_back[1], cross_back[2]], axis=1).astype(jnp.bfloat16)
    grad_pair_full = matmul_left(outer_low, grad_pair_low)
    grad_normed_out = matmul_right(grad_pair_low, pair_weight)
    grad_gain_three = jnp.sum(grad_normed_out * scaled_three, axis=0)
    grad_bias_three = jnp.sum(grad_normed_out, axis=0)
    grad_encoded = norm_back(grad_normed_out, scaled_three, root_three, vector_weight[4])
    grad_bias_middle = jnp.sum(grad_encoded, axis=0)
    grad_encoded_low = grad_encoded.astype(jnp.bfloat16)
    grad_contract_enc = matmul_left(hidden_low, grad_encoded_low)
    grad_hidden = matmul_right(grad_encoded_low, contract_full[0]) * gelu_slope(hidden_pre)
    grad_hidden_enc = jnp.sum(grad_hidden, axis=0)
    grad_hidden_low = grad_hidden.astype(jnp.bfloat16)
    grad_expand_enc = matmul_left(middle_low, grad_hidden_low)
    grad_middle = matmul_right(grad_hidden_low, expand_full[0])
    grad_gain_two = jnp.sum(grad_middle * scaled_two, axis=0)
    grad_bias_two = jnp.sum(grad_middle, axis=0)
    grad_first = grad_encoded + norm_back(grad_middle, scaled_two, root_two, vector_weight[2])
    grad_first_low = grad_first.astype(jnp.bfloat16)
    grad_out_self = matmul_left(attended_low, grad_first_low)
    grad_attended = matmul_right(grad_first_low, square_full[3]).astype(jnp.bfloat16)
    self_back = galerkin_backward(
        grad_attended,
        queries_low,
        keys_masked,
        values_low,
        self_summary,
        onehot,
        mask_float,
        self_reducer,
    )
    grad_queries = rotate_back(self_back[0].reshape(rows, H, E), cosine, sine).reshape(rows, width)
    grad_keys = rotate_back(self_back[1].reshape(rows, H, E), cosine, sine).reshape(rows, width)
    grad_joint_low = jnp.concatenate([grad_queries, grad_keys, self_back[2]], axis=1).astype(
        jnp.bfloat16
    )
    grad_joint_full = matmul_left(normed_low, grad_joint_low)
    grad_normed = matmul_right(grad_joint_low, joint_weight)
    grad_gain_one = jnp.sum(grad_normed * scaled_one, axis=0)
    grad_bias_one = jnp.sum(grad_normed, axis=0)
    grad_inputs = grad_first + norm_back(grad_normed, scaled_one, root_one, vector_weight[0])
    grad_square = jnp.stack(
        [
            grad_joint_full[:, :width],
            grad_joint_full[:, width : 2 * width],
            grad_joint_full[:, 2 * width :],
            grad_out_self,
            grad_pair_full[:, :width],
            grad_pair_full[:, width:],
            grad_out_cross,
        ]
    ).reshape(7, width * width)
    grad_expand = jnp.stack([grad_expand_enc, grad_expand_spread]).reshape(2, width * F)
    grad_contract = jnp.stack([grad_contract_enc, grad_contract_spread]).reshape(2, F * width)
    grad_fourier = grad_fourier_full.reshape(FOUR * width)
    grad_vector = jnp.stack(
        [
            grad_gain_one,
            grad_bias_one,
            grad_gain_two,
            grad_bias_two,
            grad_gain_three,
            grad_bias_three,
            grad_bias_middle,
            grad_bias_end,
        ]
    )
    grad_hidden_rows = jnp.stack([grad_hidden_enc, grad_hidden_spread])
    totals = lax.psum(
        (grad_square, grad_expand, grad_contract, grad_fourier, grad_vector, grad_hidden_rows),
        "pts",
    )
    squares = sum((jnp.sum(total_part * total_part) for total_part in totals))
    start_index = lax.axis_index("pts")
    share_square = own_share(totals[0], square_weight.shape[1], 1, start_index)
    share_expand = own_share(totals[1], expand_weight.shape[1], 1, start_index)
    share_contract = own_share(totals[2], contract_weight.shape[1], 1, start_index)
    share_fourier = own_share(totals[3], fourier_weight.shape[0], 0, start_index)
    vector_total = totals[4]
    hidden_total = totals[5]
    grad_norm = jnp.sqrt(squares)
    factor = jnp.minimum(1.0, CLIP_NORM / (grad_norm + 1e-06))
    new_square = adam_update(
        square_weight, square_first, square_second, share_square, factor, RATE_MATRIX
    )
    new_expand = adam_update(
        expand_weight, expand_first, expand_second, share_expand, factor, RATE_MATRIX
    )
    new_contract = adam_update(
        contract_weight, contract_first, contract_second, share_contract, factor, RATE_MATRIX
    )
    new_fourier = adam_update(
        fourier_weight, fourier_first, fourier_second, share_fourier, factor, RATE_MATRIX
    )
    new_vector = adam_update(
        vector_weight, vector_first, vector_second, vector_total, factor, RATE_VECTOR
    )
    new_hidden = adam_update(
        hidden_weight, hidden_first, hidden_second, hidden_total, factor, RATE_VECTOR
    )
    return (
        output.astype(jnp.bfloat16),
        grad_inputs,
        grad_norm,
        new_square[0],
        new_square[1],
        new_square[2],
        new_expand[0],
        new_expand[1],
        new_expand[2],
        new_contract[0],
        new_contract[1],
        new_contract[2],
        new_fourier[0],
        new_fourier[1],
        new_fourier[2],
        new_vector[0],
        new_vector[1],
        new_vector[2],
        new_hidden[0],
        new_hidden[1],
        new_hidden[2],
    )


def solution(mesh):
    in_specs = (
        P("pts", None),
        P(None, "pts"),
        P(),
        P("pts"),
        P("pts"),
        P("pts", None),
        P(None, "pts"),
        P(None, "pts"),
        P(None, "pts"),
        P(None, "pts"),
        P(None, "pts"),
        P(None, "pts"),
        P(None, "pts"),
        P(None, "pts"),
        P(None, "pts"),
        P("pts"),
        P("pts"),
        P("pts"),
        P(),
        P(),
        P(),
        P(),
        P(),
        P(),
    )
    out_specs = (
        P("pts", None),
        P("pts", None),
        P(),
        P(None, "pts"),
        P(None, "pts"),
        P(None, "pts"),
        P(None, "pts"),
        P(None, "pts"),
        P(None, "pts"),
        P(None, "pts"),
        P(None, "pts"),
        P(None, "pts"),
        P("pts"),
        P("pts"),
        P("pts"),
        P(),
        P(),
        P(),
        P(),
        P(),
        P(),
    )
    return jax.shard_map(shards, mesh=mesh, in_specs=in_specs, out_specs=out_specs, check_vma=False)
```

profile of v0, /device:TPU:0, one launch (start us, length us, event | category | flops | bytes accessed | tf_op | source)
XLA Modules:
  0.0 1106.9 jit_solution(6232179797096474835)
XLA Ops:
  12.7 46.2 %all_gather.12 = bf16[7,65536]{1,0:T(8,128)(2,1)S(1)} all-gather(bf16[7,2048]{1,0:T(8,128)(2,1)S(1)} %convert_element_type.146), channel_id=1, replica_groups=mesh['pts'=32] {'pts'}, dimensions={1}, use_global_device_ids=true | all-gather | bytes 946176 | tf_op jit(solution)/shard_map/all_gather | solution.py:216
  75.4 5.9 fusion.35
  99.4 5.7 fusion.50
  105.1 37.1 %psum.78 = f32[16]{0:T(128)S(1)} all-reduce(f32[16]{0:T(128)S(1)} %convolution_bitcast_fusion.5), channel_id=1, replica_groups=mesh['pts'=32] {'pts'}, use_global_device_ids=true, to_apply=%region_4.0 | all-reduce | flops 16 | bytes 128 | tf_op jit(solution)/shard_map/psum | solution.py:252
  143.3 41.7 %all_gather.14 = bf16[2,131072]{1,0:T(2,128)(2,1)S(1)} all-gather(bf16[2,4096]{1,0:T(2,128)(2,1)S(1)} %convert_element_type.158), channel_id=1, replica_groups=mesh['pts'=32] {'pts'}, dimensions={1}, use_global_device_ids=true | all-gather | bytes 540672 | tf_op jit(solution)/shard_map/all_gather | solution.py:218
  188.5 38.3 %all_gather.13 = bf16[2,131072]{1,0:T(2,128)(2,1)S(1)} all-gather(bf16[2,4096]{1,0:T(2,128)(2,1)S(1)} %convert_element_type.156), channel_id=1, replica_groups=mesh['pts'=32] {'pts'}, dimensions={1}, use_global_device_ids=true | all-gather | bytes 540672 | tf_op jit(solution)/shard_map/all_gather | solution.py:217
  237.2 38.9 %all_gather.15 = bf16[32768]{0:T(1024)(128)(2,1)S(1)} all-gather(bf16[1024]{0:T(1024)(128)(2,1)S(1)} %convert_element_type.162), channel_id=1, replica_groups=mesh['pts'=32] {'pts'}, dimensions={0}, use_global_device_ids=true | all-gather | bytes 67584 | tf_op jit(solution)/shard_map/all_gather | solution.py:219
  332.0 6.5 copy.214
  338.5 106.6 %all-reduce.10.cloned.1.call-done = f32[16,8,32,32]{3,0,2,1:T(8,128)} async-done(((f32[16,8,32,32]{3,0,2,1:T(8,128)}), f32[16,8,32,32]{3,0,2,1:T(8,128)}) %all-reduce.10.cloned.1.call-update) | async-done | bytes 524304 | tf_op jit(solution)/shard_map/psum | solution.py:273
  457.0 6.4 fusion.190
  506.9 127.5 %all-reduce.12.cloned.1.call-done = f32[16,8,32,32]{3,0,2,1:T(8,128)} async-done(((f32[16,8,32,32]{3,0,2,1:T(8,128)}), f32[16,8,32,32]{3,0,2,1:T(8,128)}) %all-reduce.12.cloned.1.call-update) | async-done | bytes 524304 | tf_op jit(solution)/shard_map/psum | solution.py:283
  675.2 7.4 convolution_bitcast_fusion.4
  682.7 6.7 fusion.191
  695.1 6.0 copy.197
  714.0 6.2 fusion.84
  743.1 123.6 %all-reduce.14.cloned.1.call-done = f32[16,8,32,32]{3,0,2,1:T(8,128)} async-done(((f32[16,8,32,32]{3,0,2,1:T(8,128)}), f32[16,8,32,32]{3,0,2,1:T(8,128)}) %all-reduce.14.cloned.1.call-update) | async-done | bytes 524304 | tf_op jit(solution)/shard_map/psum | solution.py:284
  870.4 5.7 copy.210
  897.2 13.1 %fusion.37 = (bf16[4096,256]{0,1:T(8,128)(2,1)}, bf16[4096,256]{0,1:T(8,128)(2,1)}) fusion(f32[32,8,32,128]{3,2,1,0:T(8,128)S(1)} %bitcast.342, f32[4096,8,32]{0,2,1:T(8,128)} %pad_maximum_fusion.2, f32[4096,32]{0,1:T(8,128)S(1)} %copy-done.38, f32[4096,8,32]{0,2,1:T(8,128)} %pad_maximum_fusion.3, f32[4096]{0:T(1024)S(1)} %copy-done.51, ...), kind=kLoop, calls=%fused_computation.59 | loop fusion | flops 7340032 | bytes 21512192 | tf_op jit(solution)/shard_map/convert
  910.3 5.7 fusion.54
  928.3 5.9 stack.85
  938.3 6.0 fusion.29
  944.3 5.7 copy.222
  950.2 39.8 %all-reduce = (f32[8,256]{1,0:T(8,128)S(1)}, f32[2,512]{1,0:T(2,128)S(1)}) all-reduce(f32[8,256]{1,0:T(8,128)S(1)} %stack.100, f32[2,512]{1,0:T(2,128)S(1)} %pad_maximum_fusion.14), channel_id=1, replica_groups=mesh['pts'=32] {'pts'}, use_global_device_ids=true, to_apply=%region_34.0 | all-reduce | flops 3072 | bytes 24576 | tf_op jit(solution)/shard_map/psum | solution.py:373
  991.2 86.5 %all-reduce.16.cloned.1.call-done = (f32[7,65536]{1,0:T(8,128)}, f32[2,131072]{1,0:T(2,128)}, f32[2,131072]{1,0:T(2,128)}, f32[32768]{0:T(1024)}) async-done(((f32[7,65536]{1,0:T(8,128)}, f32[2,131072]{1,0:T(2,128)}, f32[2,131072]{1,0:T(2,128)}, f32[32768]{0:T(1024)}), (f32[7,65536]{1,0:T(8,128)}, f32[2,131072]{1,0:T(2,128)}, f32[2,131072]{1,0:T(2,128)}, f32[32768]{0:T(1024)})) %all-reduce.16.cloned.1.call-update) | async-done | bytes 4063248 | tf_op jit(solution)/shard_map/psum | solution.py:373
  (404 shorter events, 306.9 us)
Async XLA Ops:
  7.2 276.6 %all-reduce.8.cloned.1.call-start = ((), (), s32[]{:S(2)}) async-start(), calls=%async_computation | async-start | bytes 4194304 | tf_op jit(solution)/shard_map/psum | solution.py:252
  67.5 224.9 %copy-start.3 = (bf16[4096,256]{0,1:T(8,128)(2,1)}, bf16[4096,256]{0,1:T(8,128)(2,1)S(1)}, u32[]{:S(2)}) copy-start(bf16[4096,256]{0,1:T(8,128)(2,1)S(1)} %copy.171) | copy-start | bytes 6291460
  105.1 340.1 %all-reduce.10.cloned.1.call-start = ((), (), s32[]{:S(2)}) async-start(), calls=%async_computation.1 | async-start | bytes 4194304 | tf_op jit(solution)/shard_map/psum | solution.py:273
  315.1 319.2 %all-reduce.12.cloned.1.call-start = ((), (), s32[]{:S(2)}) async-start(), calls=%async_computation.2 | async-start | bytes 4194304 | tf_op jit(solution)/shard_map/psum | solution.py:283
  501.5 365.2 %all-reduce.14.cloned.1.call-start = ((), (), s32[]{:S(2)}) async-start(), calls=%async_computation.3 | async-start | bytes 4194304 | tf_op jit(solution)/shard_map/psum | solution.py:284
  733.9 343.9 %all-reduce.16.cloned.1.call-start = ((), (), s32[]{:S(2)}) async-start(), calls=%async_computation.4 | async-start | bytes 8650752 | tf_op jit(solution)/shard_map/psum | solution.py:373
  950.0 141.8 %copy-start.74 = (f32[2,4096]{1,0:T(2,128)S(1)}, f32[2,4096]{1,0:T(2,128)}, u32[]{:S(2)}) copy-start(f32[2,4096]{1,0:T(2,128)} %param.33) | copy-start | bytes 98308
  950.0 141.8 %copy-start.81 = (f32[2,4096]{1,0:T(2,128)S(1)}, f32[2,4096]{1,0:T(2,128)}, u32[]{:S(2)}) copy-start(f32[2,4096]{1,0:T(2,128)} %param.35) | copy-start | bytes 98308
  950.0 141.8 %copy-start.82 = (f32[2,4096]{1,0:T(2,128)S(1)}, f32[2,4096]{1,0:T(2,128)}, u32[]{:S(2)}) copy-start(f32[2,4096]{1,0:T(2,128)} %param.34) | copy-start | bytes 98308
  950.0 143.3 %copy-start.76 = (f32[2,4096]{1,0:T(2,128)S(1)}, f32[2,4096]{1,0:T(2,128)}, u32[]{:S(2)}) copy-start(f32[2,4096]{1,0:T(2,128)} %param.36) | copy-start | bytes 98308
  950.0 143.3 %copy-start.83 = (f32[2,4096]{1,0:T(2,128)S(1)}, f32[2,4096]{1,0:T(2,128)}, u32[]{:S(2)}) copy-start(f32[2,4096]{1,0:T(2,128)} %param.38) | copy-start | bytes 98308
  950.0 143.3 %copy-start.84 = (f32[2,4096]{1,0:T(2,128)S(1)}, f32[2,4096]{1,0:T(2,128)}, u32[]{:S(2)}) copy-start(f32[2,4096]{1,0:T(2,128)} %param.37) | copy-start | bytes 98308
  950.1 144.8 %copy-start.92 = (f32[2,512]{1,0:T(2,128)S(1)}, f32[2,512]{1,0:T(2,128)}, u32[]{:S(2)}) copy-start(f32[2,512]{1,0:T(2,128)} %param.45) | copy-start | bytes 12292
  950.1 144.8 %copy-start.104 = (f32[2,512]{1,0:T(2,128)S(1)}, f32[2,512]{1,0:T(2,128)}, u32[]{:S(2)}) copy-start(f32[2,512]{1,0:T(2,128)} %param.47) | copy-start | bytes 12292
  950.1 144.8 %copy-start.105 = (f32[2,512]{1,0:T(2,128)S(1)}, f32[2,512]{1,0:T(2,128)}, u32[]{:S(2)}) copy-start(f32[2,512]{1,0:T(2,128)} %param.46) | copy-start | bytes 12292
  950.1 145.4 %copy-start.85 = (f32[8,256]{1,0:T(8,128)S(1)}, f32[8,256]{1,0:T(8,128)}, u32[]{:S(2)}) copy-start(f32[8,256]{1,0:T(8,128)} %param.42) | copy-start | bytes 24580
  950.1 145.4 %copy-start.101 = (f32[8,256]{1,0:T(8,128)S(1)}, f32[8,256]{1,0:T(8,128)}, u32[]{:S(2)}) copy-start(f32[8,256]{1,0:T(8,128)} %param.44) | copy-start | bytes 24580
  950.1 145.4 %copy-start.102 = (f32[8,256]{1,0:T(8,128)S(1)}, f32[8,256]{1,0:T(8,128)}, u32[]{:S(2)}) copy-start(f32[8,256]{1,0:T(8,128)} %param.43) | copy-start | bytes 24580
  950.1 146.0 %copy-start.65 = (f32[7,2048]{1,0:T(8,128)S(1)}, f32[7,2048]{1,0:T(8,128)}, u32[]{:S(2)}) copy-start(f32[7,2048]{1,0:T(8,128)} %param.30) | copy-start | bytes 172036
  950.1 146.0 %copy-start.77 = (f32[7,2048]{1,0:T(8,128)S(1)}, f32[7,2048]{1,0:T(8,128)}, u32[]{:S(2)}) copy-start(f32[7,2048]{1,0:T(8,128)} %param.32) | copy-start | bytes 172036
  950.1 146.0 %copy-start.78 = (f32[7,2048]{1,0:T(8,128)S(1)}, f32[7,2048]{1,0:T(8,128)}, u32[]{:S(2)}) copy-start(f32[7,2048]{1,0:T(8,128)} %param.31) | copy-start | bytes 172036
  950.2 147.5 %copy-start.93 = (f32[1024]{0:T(1024)S(1)}, f32[1024]{0:T(1024)}, u32[]{:S(2)}) copy-start(f32[1024]{0:T(1024)} %param.39) | copy-start | bytes 12292
  950.2 147.5 %copy-start.106 = (f32[1024]{0:T(1024)S(1)}, f32[1024]{0:T(1024)}, u32[]{:S(2)}) copy-start(f32[1024]{0:T(1024)} %param.41) | copy-start | bytes 12292
  950.2 147.5 %copy-start.107 = (f32[1024]{0:T(1024)S(1)}, f32[1024]{0:T(1024)}, u32[]{:S(2)}) copy-start(f32[1024]{0:T(1024)} %param.40) | copy-start | bytes 12292
  (95 other events, 1146.5 us)
Sparse Core Ops, SparseCore 0:
  105.2 130.8 all-reduce.7
  315.2 129.8 all-reduce.9
  501.6 132.6 all-reduce.11
  734.0 132.6 all-reduce.13
  934.4 143.3 all-reduce.15
where the time goes:
time: 1120 us; the launch traced here: 1110 us
  waiting for transfers between devices  444 us (40%)
  blocking collectives  242 us (22%)
  matrix products  161 us (14%)
  local copies, waits for them, and re-layouts  133 us (12%)
  other arithmetic  105 us (9%)
  between operations  21 us (2%)
    psum x2, waiting for transfers between devices, shards(): lax.psum(table_part, 'pts')  251 us
    psum x1, waiting for transfers between devices, shards(): cross_items = scale_round(lax.psum(cross_local, 'pts'), inverse_count)  107 us
    psum x1, waiting for transfers between devices, shards(): lax.psum((grad_square, grad_expand, grad_contract, grad_fourier, grad_vec...  86.5 us
    all_gather x1, blocking collectives, shards(): lax.all_gather(square_weight.astype(jnp.bfloat16), 'pts', axis=1, tiled=T...  46.2 us
    all_gather x1, blocking collectives, shards(): lax.all_gather(contract_weight.astype(jnp.bfloat16), 'pts', axis=1, tiled...  41.7 us
    psum x1, blocking collectives, shards(): lax.psum((grad_square, grad_expand, grad_contract, grad_fourier, grad_vec...  39.8 us
    all_gather x1, blocking collectives, shards(): lax.all_gather(fourier_weight.astype(jnp.bfloat16), 'pts', axis=0, tiled=...  38.9 us
    unnamed x257, local copies, waits for them, and re-layouts  38.7 us
  transfers between devices with their start and end apart: 5, of which 4 were waited for; matrix products, arithmetic and copies ran while one was open for 7% of the time, Pallas kernels for 0%

commit v1 on v0

--- a/solution.py
+++ b/solution.py
@@ -1,8 +1,12 @@
+import functools
 import math
+import types
 
 import jax
 import jax.numpy as jnp
 from jax import lax
+from jax.experimental import pallas as pl
+from jax.experimental.pallas import tpu as pltpu
 from jax.sharding import PartitionSpec as P
 
 H = 8
@@ -181,7 +185,7 @@
     return lax.dynamic_slice_in_dim(full, start_index * width, width, along)
 
 
-def shards(
+def plain(
     features,
     coords,
     fourier_basis,
@@ -427,6 +431,1082 @@
     )
 
 
+GROUP = 8
+TILE = 256
+LANES = 128
+VMEM_BYTES = 64 * 1024 * 1024
+
+
+def dot(left, right):
+    return jnp.dot(left, right, preferred_element_type=jnp.float32)
+
+
+def dot_bt(left, right):
+    return lax.dot_general(
+        left, right, (((1,), (1,)), ((), ())), preferred_element_type=jnp.float32
+    )
+
+
+def dot_at(left, right):
+    return lax.dot_general(
+        left, right, (((0,), (0,)), ((), ())), preferred_element_type=jnp.float32
+    )
+
+
+def low(values):
+    return values.astype(jnp.bfloat16)
+
+
+def column_norm(values):
+    inverse = 1.0 / values.shape[0]
+    centred = values - jnp.sum(values, axis=0, keepdims=True) * inverse
+    variance = jnp.sum(centred * centred, axis=0, keepdims=True) * inverse
+    root_inv = lax.rsqrt(variance + NORM_EPS)
+    return (centred * root_inv, root_inv)
+
+
+def column_norm_back(upstream, scaled, root_inv, gain):
+    inverse = 1.0 / upstream.shape[0]
+    through = upstream * gain
+    centre = jnp.sum(through, axis=0, keepdims=True) * inverse
+    along = jnp.sum(through * scaled, axis=0, keepdims=True) * inverse
+    return root_inv * (through - centre - scaled * along)
+
+
+def gelu_both(values):
+    square = values * values
+    half = 0.5 + 0.5 * jnp.tanh(values * (GELU_C + (GELU_C * GELU_A) * square))
+    slope = half + values * (half * (1.0 - half)) * (
+        2.0 * GELU_C + (6.0 * GELU_C * GELU_A) * square
+    )
+    return (values * half, slope)
+
+
+def turn(values, cosine, sine, sign):
+    quarter = E // 4
+    first_cos, second_cos = cosine[:quarter], cosine[quarter:]
+    first_sin, second_sin = sine[:quarter] * sign, sine[quarter:] * sign
+    parts = []
+    for base in range(0, values.shape[0], E):
+        one, two, three, four = (
+            values[base + quarter * step : base + quarter * (step + 1)] for step in range(4)
+        )
+        parts += [
+            one * first_cos - two * first_sin,
+            two * first_cos + one * first_sin,
+            three * second_cos - four * second_sin,
+            four * second_cos + three * second_sin,
+        ]
+    return jnp.concatenate(parts, axis=0)
+
+
+def compress(full):
+    width = full.shape[1]
+    head = lax.broadcasted_iota(jnp.int32, (E, width), 1) // E
+    result = full[:E]
+    for index in range(1, H):
+        result = jnp.where(head == index, full[E * index : E * (index + 1)], result)
+    return result
+
+
+def lane_sum(values):
+    result = values[:, :LANES]
+    for start in range(LANES, values.shape[1], LANES):
+        result = result + values[:, start : start + LANES]
+    return result
+
+
+def remote(source, target, send_sem, recv_sem, device):
+    return pltpu.make_async_remote_copy(
+        src_ref=source,
+        dst_ref=target,
+        send_sem=send_sem,
+        recv_sem=recv_sem,
+        device_id=(device,),
+        device_id_type=pl.DeviceIdType.MESH,
+    )
+
+
+class Place:
+    def __init__(self, devices):
+        self.devices = devices
+        self.outers = devices // GROUP
+        self.me = lax.axis_index("pts")
+        self.inner = lax.rem(self.me, GROUP)
+        self.outer = lax.div(self.me, GROUP)
+        self.core = lax.rem(self.me, 2)
+        self.pair = lax.div(self.inner, 2)
+
+    def inner_at(self, step):
+        return lax.rem(self.inner + step, GROUP)
+
+    def outer_at(self, step):
+        return lax.rem(self.outer + step, self.outers)
+
+    def pair_at(self, step):
+        return lax.rem(self.pair + step, 4)
+
+    def device(self, outer, inner):
+        return outer * GROUP + inner
+
+
+class Gather:
+    def __init__(self, place, buffer, sems):
+        self.place, self.buffer = place, buffer
+        self.send, self.recv = sems
+
+    def first(self, step, start):
+        at = self.place
+        slot = self.buffer.at[at.core, at.pair, at.outer if start else at.outer_at(step)]
+        mine = self.buffer.at[at.core, at.pair, at.outer]
+        source = at.outer if start else at.outer_at(step)
+        return remote(
+            mine, slot, self.send.at[0, step], self.recv.at[0, source],
+            at.device(at.outer_at(step), at.inner),
+        )
+
+    def second(self, step, start):
+        at = self.place
+        source = at.pair if start else at.pair_at(step)
+        return remote(
+            self.buffer.at[at.core, at.pair], self.buffer.at[at.core, source],
+            self.send.at[1, step], self.recv.at[1, source],
+            at.device(at.outer, at.pair_at(step) * 2 + at.core),
+        )
+
+    def third(self, start):
+        at = self.place
+        source = at.core if start else 1 - at.core
+        return remote(
+            self.buffer.at[at.core], self.buffer.at[source], self.send.at[2, 0],
+            self.recv.at[2, 0], at.device(at.outer, at.pair * 2 + 1 - at.core),
+        )
+
+    def start_first(self):
+        for step in range(1, self.place.outers):
+            self.first(step, True).start()
+
+    def start_second(self):
+        for step in range(1, self.place.outers):
+            self.first(step, False).wait()
+        for step in range(1, 4):
+            self.second(step, True).start()
+
+    def start_third(self):
+        for step in range(1, 4):
+            self.second(step, False).wait()
+        self.third(True).start()
+
+    def finish(self):
+        self.third(False).wait()
+
+
+class TableSum:
+    def __init__(self, place, scratch):
+        self.place, self.s, self.turn = place, scratch, 0
+
+    def swap(self, step, start):
+        at, s = self.place, self.s
+        source = at.inner if start else at.inner_at(step)
+        return remote(
+            s.table_send.at[at.inner_at(step)], s.table_recv.at[source], s.sem_ts.at[0, step],
+            s.sem_tr.at[0, source], at.device(at.outer, at.inner_at(step)),
+        )
+
+    def cross(self, step, start):
+        at, s = self.place, self.s
+        source = at.outer if start else at.outer_at(step)
+        return remote(
+            s.table_part, s.table_cross.at[self.turn, source], s.sem_ts.at[1 + self.turn, step],
+            s.sem_tr.at[1 + self.turn, source],
+            at.device(at.outer_at(step), at.inner),
+        )
+
+    def share(self, step, start, result):
+        at, s = self.place, self.s
+        source = at.inner if start else at.inner_at(step)
+        return remote(
+            result.at[at.inner], result.at[source], s.sem_ts.at[3, step], s.sem_tr.at[3, source],
+            at.device(at.outer, at.inner_at(step)),
+        )
+
+    def start(self):
+        at, s = self.place, self.s
+        high = low(s.per_block[...])
+        rest = low(s.per_block[...] - high.astype(jnp.float32))
+        table = low(dot(s.spread[...], high) + dot(s.spread[...], rest))
+        for chunk in range(at.devices):
+            s.table_send[chunk % GROUP, chunk // GROUP] = table[chunk * 16 : (chunk + 1) * 16]
+        for step in range(1, GROUP):
+            self.swap(step, True).start()
+
+    def middle(self):
+        at, s = self.place, self.s
+        total = s.table_send[at.inner].astype(jnp.float32)
+        for step in range(1, GROUP):
+            self.swap(step, False).wait()
+            total = total + s.table_recv[at.inner_at(step)].astype(jnp.float32)
+        s.table_part[...] = low(total)
+        for step in range(1, at.outers):
+            self.cross(step, True).start()
+
+    def late(self, result):
+        at, s = self.place, self.s
+        total = s.table_part[...].astype(jnp.float32)
+        for step in range(1, at.outers):
+            self.cross(step, False).wait()
+            total = total + s.table_cross[self.turn, at.outer_at(step)].astype(jnp.float32)
+        for outer in range(at.outers):
+            result[at.inner, outer] = low(total[outer] * s.inverse[outer : outer + 1, :])
+        for step in range(1, GROUP):
+            self.share(step, True, result).start()
+
+    def finish(self, result):
+        for step in range(1, GROUP):
+            self.share(step, False, result).wait()
+        self.turn = 1 - self.turn
+
+
+class GradSum:
+    def __init__(self, place, scratch, key):
+        self.place = place
+        self.full, self.half, self.quarter, self.last = (
+            getattr(scratch, name + key) for name in ("full_", "half_", "quarter_", "last_")
+        )
+        self.send, self.recv = getattr(scratch, f"sem_{key}s"), getattr(scratch, f"sem_{key}r")
+
+    def swap(self):
+        at = self.place
+        return remote(
+            self.full.at[1 - at.core], self.half, self.send.at[0, 0], self.recv.at[0, 0],
+            at.device(at.outer, at.pair * 2 + 1 - at.core),
+        )
+
+    def across(self, step, start):
+        at = self.place
+        source = at.pair if start else at.pair_at(step)
+        return remote(
+            self.half.at[at.pair_at(step)], self.quarter.at[source], self.send.at[1, step],
+            self.recv.at[1, source], at.device(at.outer, at.pair_at(step) * 2 + at.core),
+        )
+
+    def along(self, step, start):
+        at = self.place
+        source = at.outer if start else at.outer_at(step)
+        return remote(
+            self.quarter.at[at.pair, at.outer_at(step)], self.last.at[source], self.send.at[2, step],
+            self.recv.at[2, source], at.device(at.outer_at(step), at.inner),
+        )
+
+    def start(self, chunk_of):
+        at = self.place
+
+        @pl.loop(0, at.devices)
+        def _(chunk):
+            inner = lax.rem(chunk, GROUP)
+            self.full[lax.rem(inner, 2), lax.div(inner, 2), lax.div(chunk, GROUP)] = low(
+                chunk_of(chunk)
+            )
+
+        self.swap().start()
+
+    def second(self):
+        at = self.place
+        self.swap().wait()
+
+        @pl.loop(0, 4)
+        def _(pair):
+            self.half[pair] = low(
+                self.full[at.core, pair].astype(jnp.float32) + self.half[pair].astype(jnp.float32)
+            )
+
+        for step in range(1, 4):
+            self.across(step, True).start()
+
+    def third(self):
+        at = self.place
+        total = self.half[at.pair].astype(jnp.float32)
+        for step in range(1, 4):
+            self.across(step, False).wait()
+            total = total + self.quarter[at.pair_at(step)].astype(jnp.float32)
+        self.quarter[at.pair] = low(total)
+        for step in range(1, at.outers):
+            self.along(step, True).start()
+
+    def finish(self):
+        at = self.place
+        total = self.quarter[at.pair, at.outer].astype(jnp.float32)
+        for step in range(1, at.outers):
+            self.along(step, False).wait()
+            total = total + self.last[at.outer_at(step)].astype(jnp.float32)
+        return total
+
+
+def layer_kernel(names, devices, *refs):
+    s = types.SimpleNamespace(**dict(zip(names, refs)))
+    at = Place(devices)
+    points, width = s.features.shape
+    tiles = points // TILE
+    blocks = points // BLOCK
+    share = width // devices
+    tile_blocks = TILE // BLOCK
+    f32 = jnp.float32
+
+    barrier = pltpu.get_barrier_semaphore()
+    for step in range(1, GROUP):
+        pl.semaphore_signal(
+            barrier, inc=1, device_id=(at.device(at.outer, at.inner_at(step)),),
+            device_id_type=pl.DeviceIdType.MESH,
+        )
+    for step in range(1, at.outers):
+        pl.semaphore_signal(
+            barrier, inc=1, device_id=(at.device(at.outer_at(step), at.inner),),
+            device_id_type=pl.DeviceIdType.MESH,
+        )
+
+    def columns(tile):
+        return pl.ds(pl.multiple_of(tile * TILE, TILE), TILE)
+
+    def block_columns(block):
+        return pl.ds(pl.multiple_of(block * BLOCK, BLOCK), BLOCK)
+
+    def column(index):
+        return s.cols[:, index : index + 1]
+
+    def hidden_column(index):
+        return jnp.concatenate([column(8 + 2 * index), column(9 + 2 * index)], axis=0)
+
+    def out_copy(tile, target, slots, sems, index):
+        slot = lax.rem(tile, 2)
+        where = pl.ds(pl.multiple_of(tile * TILE, TILE), TILE)
+        return pltpu.make_async_copy(slots.at[slot], target.at[where, :], sems.at[index, slot])
+
+    def put_out(tile, target, slots, sems, index, values):
+        @pl.when(tile >= 2)
+        def _():
+            out_copy(tile - 2, target, slots, sems, index).wait()
+
+        slots[lax.rem(tile, 2)] = values
+        out_copy(tile, target, slots, sems, index).start()
+
+    def end_out(target, slots, sems, index):
+        for tile in range(tiles - 2, tiles):
+            out_copy(tile, target, slots, sems, index).wait()
+
+    for matrix in range(7):
+        for row in range(share):
+            s.pack[matrix * share + row : matrix * share + row + 1, :] = s.square_weight[
+                matrix : matrix + 1, row * width : (row + 1) * width
+            ]
+    for matrix in range(2):
+        for half in range(2):
+            for row in range(share):
+                place = (7 + 2 * matrix + half) * share + row
+                start = row * F + half * width
+                s.pack[place : place + 1, :] = s.expand_weight[
+                    matrix : matrix + 1, start : start + width
+                ]
+        for row in range(2 * share):
+            place = (11 + 2 * matrix) * share + row
+            s.pack[place : place + 1, :] = s.contract_weight[
+                matrix : matrix + 1, row * width : (row + 1) * width
+            ]
+    s.pack[15 * share : 16 * share, :LANES] = s.fourier_weight[...]
+    s.pack[15 * share : 16 * share, LANES:] = jnp.zeros((share, LANES), f32)
+    live = s.point_mask[...].astype(f32)
+    counts = dot_bt(jnp.ones((8, LANES), jnp.bfloat16), low(live))
+    s.pack[15 * share : 15 * share + 1, LANES : LANES + blocks] = counts[:1]
+    lane = lax.broadcasted_iota(jnp.int32, (1, LANES), 1)
+    wide_block = lax.broadcasted_iota(jnp.int32, (1, E * blocks), 1) // E
+    item_row = jnp.zeros((1, LANES), f32)
+    item_wide = jnp.zeros((1, E * blocks), jnp.int32)
+    for block in range(blocks):
+        item_row = jnp.where(lane == block, s.items[block].astype(f32), item_row)
+        item_wide = jnp.where(wide_block == block, s.items[block], item_wide)
+    s.pack[15 * share + 1 : 15 * share + 2, LANES:] = item_row
+    packed = low(s.pack[...])
+    split = s.gather_one.shape[3]
+    s.gather_one[at.core, at.pair, at.outer] = packed[:split]
+    s.gather_two[at.core, at.pair, at.outer] = packed[split:]
+
+    pl.semaphore_wait(barrier, GROUP - 1 + at.outers - 1)
+    one = Gather(at, s.gather_one, (s.sem_g1s, s.sem_g1r))
+    two = Gather(at, s.gather_two, (s.sem_g2s, s.sem_g2r))
+    one.start_first()
+    two.start_first()
+
+    row_at = lax.broadcasted_iota(jnp.int32, (width, width), 0)
+    lane_at = lax.broadcasted_iota(jnp.int32, (width, width), 1)
+    s.eye[...] = jnp.where(row_at == lane_at, 1.0, 0.0).astype(jnp.bfloat16)
+    s.heads[...] = jnp.where(row_at // E == lane_at // E, 1.0, 0.0).astype(jnp.bfloat16)
+    s.small[...] = jnp.zeros(s.small.shape, f32)
+    s.small[0:8, :] = s.vector_weight[...]
+    for row in range(2):
+        for half in range(2):
+            s.small[8 + 2 * row + half : 9 + 2 * row + half, :] = s.hidden_weight[
+                row : row + 1, half * width : (half + 1) * width
+            ]
+    s.small[12:14, : FOUR // 2] = s.fourier_basis[...]
+    s.cols[...] = s.small[...].T
+    rows_wide = lax.broadcasted_iota(jnp.int32, s.spread.shape, 0)
+    lanes_wide = lax.broadcasted_iota(jnp.int32, s.spread.shape, 1)
+    s.spread[...] = jnp.where(
+        (item_wide == rows_wide // E) & (rows_wide % E == lanes_wide % E), 1.0, 0.0
+    ).astype(jnp.bfloat16)
+    s.vector_sum[...] = jnp.zeros(s.vector_sum.shape, f32)
+    for grad in (s.grad_qkv, s.grad_o, s.grad_kv, s.grad_do, s.grad_w1, s.grad_p1, s.grad_w2, s.grad_p2, s.grad_dq):
+        grad[...] = jnp.zeros(grad.shape, f32)
+    speed = (lax.broadcasted_iota(jnp.int32, (E // 4, 1), 0).astype(f32) + 1.0) * (
+        math.pi / (E // 4)
+    )
+
+    def add_sum(index, values):
+        for part in range(values.shape[0] // width):
+            s.vector_sum[index + part] += lane_sum(values[part * width : (part + 1) * width])
+
+    def features_turned(tile):
+        return dot_bt(s.eye[...], s.features[columns(tile), :])
+
+    def before(tile, _):
+        where = columns(tile)
+        scaled, root = column_norm(features_turned(tile))
+        s.root_one[0:1, where] = root
+        s.u1[:, where] = low(scaled * column(0) + column(1))
+        x_row, y_row = s.coords[0:1, where], s.coords[1:2, where]
+        angles = jnp.concatenate([speed * x_row, speed * y_row], axis=0)
+        s.cosine[:, where] = jnp.cos(angles)
+        s.sine[:, where] = jnp.sin(angles)
+        basis = s.cols[: FOUR // 2, :]
+        phases = 2.0 * math.pi * (basis[:, 12:13] * x_row + basis[:, 13:14] * y_row)
+        s.phi[:, where] = low(jnp.concatenate([jnp.cos(phases), jnp.sin(phases)], axis=0))
+        for block in range(tile_blocks):
+            s.mask[0:1, pl.ds(pl.multiple_of(tile * TILE + block * BLOCK, BLOCK), BLOCK)] = (
+                s.point_mask[pl.ds(tile * tile_blocks + block, 1), :].astype(f32)
+            )
+
+    lax.fori_loop(0, tiles // 4, before, None)
+    one.start_second()
+    lax.fori_loop(tiles // 4, tiles // 2, before, None)
+    one.start_third()
+    two.start_second()
+    lax.fori_loop(tiles // 2, tiles, before, None)
+    one.finish()
+
+    group = 16 // share
+
+    def chunk_pair(buffer, index):
+        parts = []
+        for step in range(group):
+            chunk = index * group + step
+            inner = lax.rem(chunk, GROUP)
+            parts.append(
+                buffer[lax.rem(inner, 2), lax.div(inner, 2), lax.div(chunk, GROUP)].astype(f32)
+            )
+        return parts
+
+    def join(parts, piece):
+        return low(
+            jnp.concatenate([part[piece * share : (piece + 1) * share] for part in parts], axis=0)
+        )
+
+    @pl.loop(0, devices // group)
+    def _(index):
+        parts = chunk_pair(s.gather_one, index)
+        where = pl.ds(pl.multiple_of(index * 16, 16), 16)
+        for piece in range(3):
+            s.w_qkv[where, piece * width : (piece + 1) * width] = join(parts, piece)
+        s.w_o[where, :] = join(parts, 3)
+
+    def flip(matrix):
+        return low(dot_bt(s.eye[...], matrix))
+
+    for piece in range(3):
+        s.t_qkv[piece * width : (piece + 1) * width, :] = flip(
+            s.w_qkv[:, piece * width : (piece + 1) * width]
+        )
+    s.t_o[...] = flip(s.w_o[...])
+
+    def block_product(left, right):
+        return compress(dot_bt(left, right))
+
+    def put_products(tile, left, right):
+        for block in range(tile_blocks):
+            lanes = slice(block * BLOCK, (block + 1) * BLOCK)
+            where = pl.ds(pl.multiple_of((tile * tile_blocks + block) * E, E), E)
+            s.per_block[where, :] = block_product(left[:, lanes], right[:, lanes])
+
+    def summary(table, tile, block):
+        item = s.items[tile * tile_blocks + block]
+        first = item * 2
+        inner, outer = lax.rem(first, GROUP), lax.div(first, GROUP)
+        rows = jnp.concatenate([table[inner, outer], table[inner + 1, outer]], axis=0)
+        return jnp.concatenate([rows] * H, axis=0) * s.heads[...]
+
+    def per_block(tile, function):
+        return jnp.concatenate([function(block) for block in range(tile_blocks)], axis=1)
+
+    def lanes_of(block):
+        return slice(block * BLOCK, (block + 1) * BLOCK)
+
+    def phase_a(tile, _):
+        where = columns(tile)
+        projected = dot(s.t_qkv[...], s.u1[:, where])
+        cosine, sine = s.cosine[:, where], s.sine[:, where]
+        s.q[:, where] = low(turn(projected[:width], cosine, sine, 1.0))
+        keys = low(turn(projected[width : 2 * width], cosine, sine, 1.0) * s.mask[0:1, where])
+        values = low(projected[2 * width :])
+        s.k[:, where] = keys
+        s.v[:, where] = values
+        put_products(tile, values, keys)
+
+    lax.fori_loop(0, tiles // 2, phase_a, None)
+    two.start_third()
+    lax.fori_loop(tiles // 2, tiles, phase_a, None)
+    two.finish()
+
+    def take_two(index, carried):
+        parts = chunk_pair(s.gather_two, index)
+        where = pl.ds(pl.multiple_of(index * 16, 16), 16)
+        for piece in range(2):
+            s.w_kv[where, piece * width : (piece + 1) * width] = join(parts, piece)
+            s.w_w1[where, piece * width : (piece + 1) * width] = join(parts, 3 + piece)
+            s.w_p1[where, piece * width : (piece + 1) * width] = join(parts, 5 + piece)
+        s.w_do[where, :] = join(parts, 2)
+        both = pl.ds(pl.multiple_of(index * 32, 32), 32)
+        for piece, target in ((7, s.w_w2), (9, s.w_p2)):
+            target[both, :] = low(
+                jnp.concatenate([part[piece * share : (piece + 2) * share] for part in parts], axis=0)
+            )
+        found = []
+        for outer in range(at.outers):
+            mine = lax.div(outer * GROUP + at.inner, 2).astype(f32)
+            total = carried[outer]
+            for part in parts:
+                count_row = part[11 * share : 11 * share + 1, LANES:]
+                item_at = part[11 * share + 1 : 11 * share + 2, LANES:]
+                total = total + jnp.where(item_at == mine, count_row, 0.0)
+            found.append(total)
+        s.fourier[where, :] = jnp.concatenate(
+            [part[11 * share : 12 * share, :LANES] for part in parts], axis=0
+        )
+        return tuple(found)
+
+    table_sum = TableSum(at, s)
+    table_sum.start()
+    found = lax.fori_loop(
+        0, devices // group, take_two, tuple(jnp.zeros((1, LANES), f32) for _ in range(at.outers))
+    )
+    for outer in range(at.outers):
+        s.inverse[outer : outer + 1, :] = jnp.broadcast_to(
+            1.0 / jnp.sum(found[outer], axis=1, keepdims=True), (1, width)
+        )
+    w_dq = jnp.concatenate(
+        [s.fourier[pl.ds(0, FOUR, stride=2), :], s.fourier[pl.ds(1, FOUR, stride=2), :]], axis=1
+    )
+    table_sum.middle()
+    s.t_dq[...] = low(w_dq.T)
+    for piece in range(2):
+        cols = slice(piece * width, (piece + 1) * width)
+        s.t_kv[cols, :] = flip(s.w_kv[:, cols])
+        s.t_w1[cols, :] = flip(s.w_w1[:, cols])
+        s.t_p1[cols, :] = flip(s.w_p1[:, cols])
+        s.t_w2[:, cols] = flip(s.w_w2[cols, :])
+        s.t_p2[:, cols] = flip(s.w_p2[cols, :])
+    s.t_do[...] = flip(s.w_do[...])
+    table_sum.late(s.table_self)
+
+    def cross_queries(tile, _):
+        where = columns(tile)
+        s.qd[:, where] = low(dot(s.t_dq[...], s.phi[:, where]))
+
+    lax.fori_loop(0, tiles, cross_queries, None)
+    table_sum.finish(s.table_self)
+
+    def phase_b(tile, _):
+        where = columns(tile)
+        mask = s.mask[0:1, where]
+        queries = s.q[:, where]
+        mixed = per_block(
+            tile, lambda b: dot(summary(s.table_self, tile, b), queries[:, lanes_of(b)])
+        )
+        attended = low(mixed * mask)
+        s.o[:, where] = attended
+        first_sum = features_turned(tile) + dot(s.t_o[...], attended)
+        scaled_two, root_two = column_norm(first_sum)
+        s.root_two[0:1, where] = root_two
+        s.xh2[:, where] = low(scaled_two)
+        middle = low(scaled_two * column(2) + column(3))
+        s.u2[:, where] = middle
+        hidden, slope = gelu_both(dot(s.t_w1[...], middle) + hidden_column(0))
+        hidden = low(hidden)
+        s.e1[:, where] = hidden
+        s.slope[:, where] = low(slope)
+        encoded = first_sum + dot(s.t_w2[...], hidden) + column(6)
+        scaled_three, root_three = column_norm(encoded)
+        s.root_three[0:1, where] = root_three
+        s.xh3[:, where] = low(scaled_three)
+        outer = low(scaled_three * column(4) + column(5))
+        s.u3[:, where] = outer
+        pair = dot(s.t_kv[...], outer)
+        keys = low(pair[:width] * mask)
+        values = low(pair[width:])
+        s.kd[:, where] = keys
+        s.vd[:, where] = values
+        put_products(tile, values, keys)
+
+    lax.fori_loop(0, tiles, phase_b, None)
+    table_sum.start()
+    table_sum.middle()
+    table_sum.late(s.table_other)
+    table_sum.finish(s.table_other)
+
+    def phase_c(tile, _):
+        where = columns(tile)
+        mask = s.mask[0:1, where]
+        queries = s.qd[:, where]
+        tables = [summary(s.table_other, tile, block) for block in range(tile_blocks)]
+        decoded = low(
+            per_block(tile, lambda b: dot(tables[b], queries[:, lanes_of(b)])) * mask
+        )
+        latent = dot(s.t_do[...], decoded)
+        latent_low = low(latent)
+        hidden, slope = gelu_both(dot(s.t_p1[...], latent_low) + hidden_column(1))
+        hidden = low(hidden)
+        output = latent + dot(s.t_p2[...], hidden) + column(7)
+        put_out(tile, s.layer_output, s.output_slots, s.sem_out, 0, low(dot_bt(s.eye[...], low(output))))
+        upstream = s.cotangent[where, :]
+        turned = dot_bt(s.eye[...], upstream)
+        add_sum(7, turned)
+        grad_spread = dot_bt(s.w_p2[...], upstream) * slope
+        add_sum(10, grad_spread)
+        grad_spread = low(grad_spread)
+        grad_latent = low(turned + dot(s.w_p1[...], grad_spread))
+        grad_decoded = low(dot(s.w_do[...], grad_latent) * mask)
+        grad_queries = low(
+            per_block(tile, lambda b: dot_at(tables[b], grad_decoded[:, lanes_of(b)]))
+        )
+        put_products(tile, grad_decoded, queries)
+        s.grad_p2[...] += dot(hidden, upstream)
+        s.grad_p1[...] += dot_bt(latent_low, grad_spread)
+        s.grad_do[...] += dot_bt(decoded, grad_latent)
+        s.grad_dq[...] += dot_bt(s.phi[:, where], grad_queries)
+
+    lax.fori_loop(0, tiles, phase_c, None)
+    table_sum.start()
+    end_out(s.layer_output, s.output_slots, s.sem_out, 0)
+    s.fourier[pl.ds(0, FOUR, stride=2), :] = s.grad_dq[:, :LANES]
+    s.fourier[pl.ds(1, FOUR, stride=2), :] = s.grad_dq[:, LANES:]
+    zeros = jnp.zeros((share, LANES), f32)
+
+    def rows_of(chunk, count=1):
+        size = share * count
+        return pl.ds(pl.multiple_of(chunk * size, size), size)
+
+    def chunk_c(chunk):
+        where = rows_of(chunk)
+        return jnp.concatenate(
+            [
+                s.grad_do[where, :],
+                s.grad_p1[where, :width],
+                s.grad_p1[where, width:],
+                s.grad_p2[rows_of(chunk, 2), :],
+                jnp.concatenate([s.fourier[where, :], zeros], axis=1),
+            ],
+            axis=0,
+        )
+
+    sum_c = GradSum(at, s, "c")
+    sum_c.start(chunk_c)
+    table_sum.middle()
+    sum_c.second()
+    table_sum.late(s.table_other)
+    table_sum.finish(s.table_other)
+
+    def phase_d(tile, _):
+        where = columns(tile)
+        mask = s.mask[0:1, where]
+        keys, values = s.kd[:, where], s.vd[:, where]
+        tables = [summary(s.table_other, tile, block) for block in range(tile_blocks)]
+        grad_keys = per_block(tile, lambda b: dot_at(tables[b], values[:, lanes_of(b)])) * mask
+        grad_values = per_block(tile, lambda b: dot(tables[b], keys[:, lanes_of(b)]))
+        grad_pair = low(jnp.concatenate([grad_keys, grad_values], axis=0))
+        s.grad_kv[...] += dot_bt(s.u3[:, where], grad_pair)
+        grad_outer = dot(s.w_kv[...], grad_pair)
+        scaled = s.xh3[:, where].astype(f32)
+        add_sum(4, grad_outer * scaled)
+        add_sum(5, grad_outer)
+        grad_encoded = column_norm_back(
+            grad_outer, scaled, s.root_three[0:1, where], column(4)
+        )
+        add_sum(6, grad_encoded)
+        grad_encoded_low = low(grad_encoded)
+        s.grad_w2[...] += dot_bt(s.e1[:, where], grad_encoded_low)
+        grad_hidden = dot(s.w_w2[...], grad_encoded_low) * s.slope[:, where].astype(f32)
+        add_sum(8, grad_hidden)
+        grad_hidden = low(grad_hidden)
+        s.grad_w1[...] += dot_bt(s.u2[:, where], grad_hidden)
+        grad_middle = dot(s.w_w1[...], grad_hidden)
+        scaled = s.xh2[:, where].astype(f32)
+        add_sum(2, grad_middle * scaled)
+        add_sum(3, grad_middle)
+        grad_first = grad_encoded + column_norm_back(
+            grad_middle, scaled, s.root_two[0:1, where], column(2)
+        )
+        grad_first = low(grad_first)
+        s.xh2[:, where] = grad_first
+        s.grad_o[...] += dot_bt(s.o[:, where], grad_first)
+        grad_attended = low(dot(s.w_o[...], grad_first) * mask)
+        s.kd[:, where] = grad_attended
+        put_products(tile, grad_attended, s.q[:, where])
+
+    lax.fori_loop(0, tiles // 2, phase_d, None)
+    sum_c.third()
+    lax.fori_loop(tiles // 2, tiles, phase_d, None)
+    table_sum.start()
+    s.grads_c[...] = sum_c.finish()
+
+    def chunk_d(chunk):
+        where = rows_of(chunk)
+        return jnp.concatenate(
+            [
+                s.grad_kv[where, :width],
+                s.grad_kv[where, width:],
+                s.grad_o[where, :],
+                s.grad_w1[where, :width],
+                s.grad_w1[where, width:],
+                s.grad_w2[rows_of(chunk, 2), :],
+                jnp.zeros((share, width), f32),
+            ],
+            axis=0,
+        )
+
+    sum_d = GradSum(at, s, "d")
+    sum_d.start(chunk_d)
+    table_sum.middle()
+
+    def query_grads(tile, _):
+        where = columns(tile)
+        upstream = s.kd[:, where]
+        grad = per_block(
+            tile, lambda b: dot_at(summary(s.table_self, tile, b), upstream[:, lanes_of(b)])
+        )
+        grad = low(turn(grad, s.cosine[:, where], s.sine[:, where], -1.0))
+        s.q[:, where] = grad
+        s.grad_qkv[:, :width] += dot_bt(s.u1[:, where], grad)
+
+    lax.fori_loop(0, tiles // 2, query_grads, None)
+    sum_d.second()
+    table_sum.late(s.table_other)
+    lax.fori_loop(tiles // 2, tiles, query_grads, None)
+    table_sum.finish(s.table_other)
+
+    def phase_e(tile, _):
+        where = columns(tile)
+        mask = s.mask[0:1, where]
+        keys, values = s.k[:, where], s.v[:, where]
+        tables = [summary(s.table_other, tile, block) for block in range(tile_blocks)]
+        grad_keys = per_block(tile, lambda b: dot_at(tables[b], values[:, lanes_of(b)])) * mask
+        grad_values = low(per_block(tile, lambda b: dot(tables[b], keys[:, lanes_of(b)])))
+        grad_keys = low(turn(grad_keys, s.cosine[:, where], s.sine[:, where], -1.0))
+        pair = jnp.concatenate([grad_keys, grad_values], axis=0)
+        s.grad_qkv[:, width:] += dot_bt(s.u1[:, where], pair)
+        grad_normed = dot(s.w_qkv[...], jnp.concatenate([s.q[:, where], pair], axis=0))
+        turned = features_turned(tile)
+        root = s.root_one[0:1, where]
+        scaled = (turned - jnp.sum(turned, axis=0, keepdims=True) * (1.0 / width)) * root
+        add_sum(0, grad_normed * scaled)
+        add_sum(1, grad_normed)
+        grad_input = s.xh2[:, where].astype(f32) + column_norm_back(
+            grad_normed, scaled, root, column(0)
+        )
+        put_out(tile, s.input_grad, s.input_slots, s.sem_out, 1, grad_input.T)
+
+    lax.fori_loop(0, tiles // 2, phase_e, None)
+    sum_d.third()
+    lax.fori_loop(tiles // 2, tiles, phase_e, None)
+
+    lane_wide = lax.broadcasted_iota(jnp.int32, (width, LANES), 1)
+    sums = jnp.zeros((width, LANES), f32)
+    for index in range(12):
+        sums = jnp.where(
+            lane_wide == index, jnp.sum(s.vector_sum[index], axis=1, keepdims=True), sums
+        )
+    s.vector_cols[...] = sums
+
+    def chunk_e(chunk):
+        where = rows_of(chunk)
+        return jnp.concatenate(
+            [
+                s.grad_qkv[where, :width],
+                s.grad_qkv[where, width : 2 * width],
+                s.grad_qkv[where, 2 * width :],
+                jnp.concatenate([s.vector_cols[where, :], zeros], axis=1),
+            ],
+            axis=0,
+        )
+
+    sum_e = GradSum(at, s, "e")
+    sum_e.start(chunk_e)
+    s.grads_d[...] = sum_d.finish()
+    end_out(s.input_grad, s.input_slots, s.sem_out, 1)
+    sum_e.second()
+    early = jnp.sum(s.grads_c[...] * s.grads_c[...], axis=0, keepdims=True) + jnp.sum(
+        s.grads_d[...] * s.grads_d[...], axis=0, keepdims=True
+    )
+    sum_e.third()
+    grads_e = sum_e.finish()
+    s.grads_e[...] = grads_e
+    squares = jnp.sum(early + jnp.sum(grads_e * grads_e, axis=0, keepdims=True), axis=1, keepdims=True)
+    vector_rows = grads_e[3 * share : 4 * share, :LANES]
+    row_small = lax.broadcasted_iota(jnp.int32, (share, LANES), 0)
+    lane_small = lax.broadcasted_iota(jnp.int32, (share, LANES), 1)
+    s.final[at.inner, at.outer] = jnp.where(
+        (row_small == 0) & (lane_small == 12), squares, vector_rows
+    )
+
+    def final_along(step, start):
+        source = at.outer if start else at.outer_at(step)
+        return remote(
+            s.final.at[at.inner, at.outer], s.final.at[at.inner, source], s.sem_fs.at[0, step],
+            s.sem_fr.at[0, source], at.device(at.outer_at(step), at.inner),
+        )
+
+    def final_inner(step, start):
+        source = at.inner if start else at.inner_at(step)
+        return remote(
+            s.final.at[at.inner], s.final.at[source], s.sem_fs.at[1, step],
+            s.sem_fr.at[1, source], at.device(at.outer, at.inner_at(step)),
+        )
+
+    for step in range(1, at.outers):
+        final_along(step, True).start()
+    for step in range(1, at.outers):
+        final_along(step, False).wait()
+    for step in range(1, GROUP):
+        final_inner(step, True).start()
+    for step in range(1, GROUP):
+        final_inner(step, False).wait()
+
+    @pl.loop(0, devices)
+    def _(chunk):
+        s.vector_all[rows_of(chunk), :] = s.final[lax.rem(chunk, GROUP), lax.div(chunk, GROUP)]
+
+
+def update_kernel(share, *refs):
+    grads_c, grads_d, grads_e, vector_all = refs[:4]
+    weights = refs[4:22]
+    norm_out = refs[22]
+    results = refs[23:41]
+    flat_square, flat_expand, flat_contract = refs[41:]
+    width = grads_c.shape[1]
+    places = [(grads_e, 0), (grads_e, 1), (grads_e, 2), (grads_d, 2), (grads_d, 0), (grads_d, 1), (grads_c, 0)]
+    for matrix, (source, piece) in enumerate(places):
+        for row in range(share):
+            start = piece * share + row
+            flat_square[matrix : matrix + 1, row * width : (row + 1) * width] = source[
+                start : start + 1, :
+            ]
+    for matrix, (source, piece) in enumerate(((grads_d, 3), (grads_c, 1))):
+        for half in range(2):
+            for row in range(share):
+                start = (piece + half) * share + row
+                target = row * F + half * width
+                flat_expand[matrix : matrix + 1, target : target + width] = source[
+                    start : start + 1, :
+                ]
+    for matrix, (source, piece) in enumerate(((grads_d, 5), (grads_c, 3))):
+        for row in range(2 * share):
+            start = piece * share + row
+            flat_contract[matrix : matrix + 1, row * width : (row + 1) * width] = source[
+                start : start + 1, :
+            ]
+    fourier = grads_c[5 * share : 6 * share, :LANES]
+    turned = vector_all[...].T
+    norm = jnp.sqrt(jnp.sum(turned[12:13, :], axis=1, keepdims=True))
+    norm_out[...] = norm
+    factor = jnp.minimum(1.0, CLIP_NORM / (norm + 1e-06))
+    hidden = jnp.concatenate(
+        [
+            jnp.concatenate([turned[8:9], turned[9:10]], axis=1),
+            jnp.concatenate([turned[10:11], turned[11:12]], axis=1),
+        ],
+        axis=0,
+    )
+    grads = (flat_square[...], flat_expand[...], flat_contract[...], fourier, turned[:8], hidden)
+    rates = (RATE_MATRIX,) * 4 + (RATE_VECTOR,) * 2
+    for index, (grad, rate) in enumerate(zip(grads, rates)):
+        weight, first, second = (weights[3 * index + part][...] for part in range(3))
+        values = adam_update(weight, first, second, grad, factor, rate)
+        for part in range(3):
+            results[3 * index + part][...] = values[part]
+
+
+def fused(devices, features, coords, fourier_basis, block_items, point_mask, cotangent, *weights):
+    points, width = features.shape
+    blocks = points // BLOCK
+    outers = devices // GROUP
+    share = width // devices
+    items = points * devices // ITEM_PTS
+    bf16, f32 = jnp.bfloat16, jnp.float32
+    square, expand, contract, fourier, vector, hidden = (weights[3 * i] for i in range(6))
+    vmem = lambda shape, dtype: pltpu.VMEM(shape, dtype)
+    inputs = {
+        "items": block_items,
+        "features": features,
+        "coords": coords,
+        "fourier_basis": fourier_basis,
+        "point_mask": point_mask.reshape(blocks, BLOCK),
+        "cotangent": cotangent,
+        "square_weight": square,
+        "expand_weight": expand,
+        "contract_weight": contract,
+        "fourier_weight": fourier.reshape(share, LANES),
+        "vector_weight": vector,
+        "hidden_weight": hidden,
+    }
+    rows_c, rows_d, rows_e = 6 * share, 8 * share, 4 * share
+    outputs = {
+        "layer_output": ((points, width), bf16),
+        "input_grad": ((points, width), f32),
+        "grads_c": ((rows_c, width), f32),
+        "grads_d": ((rows_d, width), f32),
+        "grads_e": ((rows_e, width), f32),
+        "vector_all": ((width, LANES), f32),
+    }
+    tall = lambda rows: vmem((rows, points), bf16)
+    scratch = {
+        "pack": vmem((16 * share, width), f32),
+        "gather_one": vmem((2, 4, outers, 4 * share, width), bf16),
+        "gather_two": vmem((2, 4, outers, 12 * share, width), bf16),
+        "eye": vmem((width, width), bf16),
+        "heads": vmem((width, width), bf16),
+        "small": vmem((LANES, width), f32),
+        "cols": vmem((width, LANES), f32),
+        "spread": vmem((items * E, blocks * E), bf16),
+        "vector_sum": vmem((12, width, LANES), f32),
+        "vector_cols": vmem((width, LANES), f32),
+        "grad_qkv": vmem((width, 3 * width), f32),
+        "grad_o": vmem((width, width), f32),
+        "grad_kv": vmem((width, 2 * width), f32),
+        "grad_do": vmem((width, width), f32),
+        "grad_w1": vmem((width, F), f32),
+        "grad_p1": vmem((width, F), f32),
+        "grad_w2": vmem((F, width), f32),
+        "grad_p2": vmem((F, width), f32),
+        "grad_dq": vmem((FOUR, width), f32),
+        "fourier": vmem((2 * FOUR, LANES), f32),
+        "w_qkv": vmem((width, 3 * width), bf16),
+        "t_qkv": vmem((3 * width, width), bf16),
+        "w_o": vmem((width, width), bf16),
+        "t_o": vmem((width, width), bf16),
+        "w_kv": vmem((width, 2 * width), bf16),
+        "t_kv": vmem((2 * width, width), bf16),
+        "w_do": vmem((width, width), bf16),
+        "t_do": vmem((width, width), bf16),
+        "w_w1": vmem((width, F), bf16),
+        "t_w1": vmem((F, width), bf16),
+        "w_p1": vmem((width, F), bf16),
+        "t_p1": vmem((F, width), bf16),
+        "w_w2": vmem((F, width), bf16),
+        "t_w2": vmem((width, F), bf16),
+        "w_p2": vmem((F, width), bf16),
+        "t_p2": vmem((width, F), bf16),
+        "t_dq": vmem((width, FOUR), bf16),
+        "mask": vmem((1, points), f32),
+        "root_one": vmem((1, points), f32),
+        "root_two": vmem((1, points), f32),
+        "root_three": vmem((1, points), f32),
+        "cosine": vmem((E // 2, points), f32),
+        "sine": vmem((E // 2, points), f32),
+        "phi": tall(FOUR),
+        "u1": tall(width),
+        "q": tall(width),
+        "k": tall(width),
+        "v": tall(width),
+        "qd": tall(width),
+        "o": tall(width),
+        "xh2": tall(width),
+        "u2": tall(width),
+        "e1": tall(F),
+        "slope": tall(F),
+        "xh3": tall(width),
+        "u3": tall(width),
+        "kd": tall(width),
+        "vd": tall(width),
+        "per_block": vmem((blocks * E, width), f32),
+        "inverse": vmem((max(8, outers), width), f32),
+        "table_send": vmem((GROUP, outers, 16, width), bf16),
+        "table_recv": vmem((GROUP, outers, 16, width), bf16),
+        "table_part": vmem((outers, 16, width), bf16),
+        "table_cross": vmem((2, outers, outers, 16, width), bf16),
+        "table_self": vmem((GROUP, outers, 16, width), bf16),
+        "table_other": vmem((GROUP, outers, 16, width), bf16),
+        "final": vmem((GROUP, outers, share, LANES), f32),
+        "output_slots": vmem((2, TILE, width), bf16),
+        "input_slots": vmem((2, TILE, width), f32),
+        "sem_out": pltpu.SemaphoreType.DMA((2, 2)),
+    }
+    for key, rows in (("c", rows_c), ("d", rows_d), ("e", rows_e)):
+        scratch["full_" + key] = vmem((2, 4, outers, rows, width), bf16)
+        for part in ("half_", "quarter_"):
+            scratch[part + key] = vmem((4, outers, rows, width), bf16)
+        scratch["last_" + key] = vmem((outers, rows, width), bf16)
+    many = max(GROUP, outers)
+    for key in ("ts", "tr", "g1s", "g1r", "g2s", "g2r", "cs", "cr", "ds", "dr", "es", "er"):
+        scratch["sem_" + key] = pltpu.SemaphoreType.DMA((4, many))
+    for key in ("fs", "fr"):
+        scratch["sem_" + key] = pltpu.SemaphoreType.DMA((2, many))
+    names = list(inputs) + list(outputs) + list(scratch)
+    in_specs = [pl.BlockSpec(memory_space=pltpu.SMEM)] + [
+        pl.BlockSpec(memory_space=pltpu.VMEM) for _ in range(len(inputs) - 1)
+    ]
+    whole = pl.BlockSpec(memory_space=pltpu.VMEM)
+    made = pl.pallas_call(
+        functools.partial(layer_kernel, names, devices),
+        out_shape=[jax.ShapeDtypeStruct(*shape) for shape in outputs.values()],
+        in_specs=in_specs,
+        out_specs=[pl.BlockSpec(memory_space=pl.ANY)] * 2 + [whole] * (len(outputs) - 2),
+        scratch_shapes=list(scratch.values()),
+        compiler_params=pltpu.CompilerParams(
+            collective_id=0, has_side_effects=True, vmem_limit_bytes=VMEM_BYTES
+        ),
+    )(*inputs.values())
+    layer_output, input_grad, *sums = made
+    flat = list(weights)
+    for part in range(9, 12):
+        flat[part] = flat[part].reshape(share, LANES)
+    shapes = [jax.ShapeDtypeStruct((1, 1), f32)] + [
+        jax.ShapeDtypeStruct(flat[index].shape, f32) for index in range(18)
+    ]
+    order = []
+    for index in range(6):
+        order += [shapes[1 + 3 * index]] * 3
+    updated = pl.pallas_call(
+        functools.partial(update_kernel, share),
+        out_shape=[shapes[0]] + order,
+        in_specs=[whole] * 22,
+        out_specs=[whole] * 19,
+        scratch_shapes=[
+            vmem(square.shape, f32),
+            vmem(expand.shape, f32),
+            vmem(contract.shape, f32),
+        ],
+        compiler_params=pltpu.CompilerParams(vmem_limit_bytes=16 * 1024 * 1024),
+    )(*sums, *flat)
+    norm, *rest = updated
+    for part in range(9, 12):
+        rest[part] = rest[part].reshape(fourier.shape)
+    return (layer_output, input_grad, norm.reshape(()), *rest)
+
+
+def shards(features, *others):
+    devices = lax.axis_size("pts")
+    width = features.shape[1]
+    if devices % GROUP == 0 and width % (8 * devices) == 0:
+        return fused(devices, features, *others)
+    return plain(features, *others)
+
+
 def solution(mesh):
     in_specs = (
         P("pts", None),

time: 1120 us -> 250 us (0.22); the launches traced: 1110 us -> 249 us
  waiting for transfers between devices: 444 us -> 0 us
  blocking collectives: 242 us -> 0 us
  Pallas kernels: 0 us -> 227 us
  matrix products: 161 us -> 0 us
  local copies, waits for them, and re-layouts: 133 us -> 21.8 us
  other arithmetic: 105 us -> 0 us
  between operations: 21 us -> 0.71 us
    psum x5 -> x0, waiting for transfers between devices: 444 us -> none  [the longest x2 251 us: shards(): lax.psum(table_part, 'pts')]
    pallas_call x0 -> x2, Pallas kernels: none -> 227 us  [the longest x1 226 us: fused(): pl.pallas_call(functools.partial(layer_kernel, names, devices), out_shape...]
    all_gather x4 -> x0, blocking collectives: 165 us -> none  [the longest x1 46.2 us: shards(): lax.all_gather(square_weight.astype(jnp.bfloat16), 'pts', axis=1, tiled=T...]
    dot_general x47 -> x0, matrix products: 161 us -> none  [the longest x9 30.3 us: matmul_left(): lax.dot_general(left, right, (((0,), (0,)), ((), ())), preferred_element_...]
    psum x2 -> x0, blocking collectives: 76.9 us -> none  [the longest x1 39.8 us: shards(): lax.psum((grad_square, grad_expand, grad_contract, grad_fourier, grad_vec...]
    reduce_sum x16 -> x0, other arithmetic: 33.3 us -> none  [the longest x6 11.3 us: shards(): squares = sum((jnp.sum(total_part * total_part) for total_part in totals))]
    transpose x7 -> x0, local copies, waits for them, and re-layouts: 24.9 us -> none  [apply_summary(): jnp.einsum(pattern, rows_low.reshape(blocks, BLOCK, H, E), block_summary,...]
    another operation x6 -> x0, other arithmetic: 24.1 us -> none
  transfers between devices with their start and end apart: 5 -> 0, of which waited for: 4 -> 0; matrix products, arithmetic and copies ran while one was open for 7% -> 0% of each run, Pallas kernels for 0% -> 0%
where the time goes in v1:
time: 250 us; the launch traced here: 249 us
  Pallas kernels  227 us (91%)
  local copies, waits for them, and re-layouts  21.8 us (9%)
    pallas_call x1, Pallas kernels, fused(): pl.pallas_call(functools.partial(layer_kernel, names, devices), out_shape...  226 us
    unnamed x48, local copies, waits for them, and re-layouts  21.8 us

profile of v1, /device:TPU:0, one launch (start us, length us, event | category | flops | bytes accessed | tf_op | source)
XLA Modules:
  0.0 249.2 jit_solution(4787790671569378825)
XLA Ops:
  0.7 225.8 %shard_map.391 = (bf16[4096,256]{1,0:T(8,128)(2,1)}, f32[4096,256]{1,0:T(8,128)}, f32[48,256]{1,0:T(8,128)}, f32[64,256]{1,0:T(8,128)}, f32[32,256]{1,0:T(8,128)}, /*index=5*/f32[256,128]{1,0:T(8,128)}) custom-call(s32[32]{0:T(128)} %refs_0_.1, bf16[4096,256]{1,0:T(8,128)(2,1)} %refs_1_.1, f32[2,4096]{1,0:T(2,128)} %refs_2_.1, f32[2,64]{1,0:T(2,128)} %refs_3_.1, ...), custom_call_target="tpu_custom_call" | custom-call | tf_op jit(solution)/shard_map/pallas_call | solution.py:1464
  226.4 0.8 copy-done
  227.3 0.8 copy-done.1
  228.0 0.8 copy-done.2
  228.8 0.9 copy-done.3
  229.7 0.8 copy-done.4
  230.5 0.8 copy-done.5
  231.4 0.8 copy-done.6
  232.2 0.8 copy-done.7
  233.0 0.7 copy-done.8
  233.7 0.8 copy-done.9
  234.5 0.8 copy-done.10
  235.2 0.8 copy-done.11
  236.0 0.8 copy-done.12
  236.7 0.8 copy-done.13
  237.5 0.7 copy-done.14
  238.9 0.7 copy-done.16
  239.6 0.7 copy-done.17
  240.3 0.7 copy-done.18
  241.0 0.7 copy-done.19
  242.3 0.7 copy-done.21
  243.0 1.0 shard_map.392
  244.0 3.2 %copy.47 = bf16[4096,256]{1,0:T(8,128)(2,1)} copy(bf16[4096,256]{1,0:T(8,128)(2,1)} %get-tuple-element.92) | data formatting | bytes 4194304
  247.2 2.0 copy.48
  (26 shorter events, 1.4 us)
Async XLA Ops:
  226.4 0.8 copy-start
  227.3 0.8 copy-start.1
  228.0 0.8 copy-start.2
  228.8 0.9 copy-start.3
  229.7 0.8 copy-start.4
  230.5 0.8 copy-start.5
  231.4 0.8 copy-start.6
  232.2 0.8 copy-start.7
  233.0 0.7 copy-start.8
  233.7 0.8 copy-start.9
  234.5 0.8 copy-start.10
  235.2 0.8 copy-start.11
  236.0 0.8 copy-start.12
  236.7 0.8 copy-start.13
  237.5 0.7 copy-start.14
  238.2 0.7 copy-start.15
  238.9 0.7 copy-start.16
  239.6 0.7 copy-start.17
  240.3 0.7 copy-start.18
  241.0 0.7 copy-start.19
  241.6 0.7 copy-start.20
  242.3 0.7 copy-start.21
  244.0 3.2 %copy-start.22 = (f32[4096,256]{1,0:T(8,128)S(1)}, f32[4096,256]{1,0:T(8,128)}, u32[]{:S(2)}) copy-start(f32[4096,256]{1,0:T(8,128)} %get-tuple-element.93) | copy-start | bytes 12582916

commit v2 on v1

--- a/solution.py
+++ b/solution.py
@@ -432,8 +432,9 @@
 
 
 GROUP = 8
-TILE = 256
+TILE = 512
 LANES = 128
+PIECES = 8
 VMEM_BYTES = 64 * 1024 * 1024
 
 
@@ -668,11 +669,12 @@
 
 
 class GradSum:
-    def __init__(self, place, scratch, key):
+    def __init__(self, place, scratch, key, first):
         self.place = place
-        self.full, self.half, self.quarter, self.last = (
-            getattr(scratch, name + key) for name in ("full_", "half_", "quarter_", "last_")
-        )
+        self.half, self.quarter, self.last = (
+            getattr(scratch, name + key) for name in ("half_", "quarter_", "last_")
+        )
+        self.full = scratch.gather_two.at[:, :, :, first : first + self.last.shape[1]]
         self.send, self.recv = getattr(scratch, f"sem_{key}s"), getattr(scratch, f"sem_{key}r")
 
     def swap(self):
@@ -1073,7 +1075,7 @@
         hidden, slope = gelu_both(dot(s.t_p1[...], latent_low) + hidden_column(1))
         hidden = low(hidden)
         output = latent + dot(s.t_p2[...], hidden) + column(7)
-        put_out(tile, s.layer_output, s.output_slots, s.sem_out, 0, low(dot_bt(s.eye[...], low(output))))
+        put_out(tile, s.layer_output, s.output_slots, s.sem_out, 0, low(output).T)
         upstream = s.cotangent[where, :]
         turned = dot_bt(s.eye[...], upstream)
         add_sum(7, turned)
@@ -1115,7 +1117,7 @@
             axis=0,
         )
 
-    sum_c = GradSum(at, s, "c")
+    sum_c = GradSum(at, s, "c", 0)
     sum_c.start(chunk_c)
     table_sum.middle()
     sum_c.second()
@@ -1180,7 +1182,7 @@
             axis=0,
         )
 
-    sum_d = GradSum(at, s, "d")
+    sum_d = GradSum(at, s, "d", 0)
     sum_d.start(chunk_d)
     table_sum.middle()
 
@@ -1245,7 +1247,7 @@
             axis=0,
         )
 
-    sum_e = GradSum(at, s, "e")
+    sum_e = GradSum(at, s, "e", 8 * share)
     sum_e.start(chunk_e)
     s.grads_d[...] = sum_d.finish()
     end_out(s.input_grad, s.input_slots, s.sem_out, 1)
@@ -1293,11 +1295,23 @@
 
 
 def update_kernel(share, *refs):
+    sources, refs = refs[:2], refs[2:]
     grads_c, grads_d, grads_e, vector_all = refs[:4]
     weights = refs[4:22]
-    norm_out = refs[22]
-    results = refs[23:41]
-    flat_square, flat_expand, flat_contract = refs[41:]
+    targets = refs[22:24]
+    norm_out = refs[24]
+    results = refs[25:43]
+    flat_square, flat_expand, flat_contract, *held, sems = refs[43:]
+    loads, stores = [], []
+    for index, (source, target) in enumerate(zip(sources, targets)):
+        size = source.shape[0] // PIECES
+        for piece in range(PIECES):
+            where = slice(piece * size, (piece + 1) * size)
+            own = held[index].at[where]
+            loads.append(pltpu.make_async_copy(source.at[where], own, sems.at[0, index, piece]))
+            stores.append(pltpu.make_async_copy(own, target.at[where], sems.at[1, index, piece]))
+    for load in loads:
+        load.start()
     width = grads_c.shape[1]
     places = [(grads_e, 0), (grads_e, 1), (grads_e, 2), (grads_d, 2), (grads_d, 0), (grads_d, 1), (grads_c, 0)]
     for matrix, (source, piece) in enumerate(places):
@@ -1320,6 +1334,9 @@
             flat_contract[matrix : matrix + 1, row * width : (row + 1) * width] = source[
                 start : start + 1, :
             ]
+    for load, store in zip(loads, stores):
+        load.wait()
+        store.start()
     fourier = grads_c[5 * share : 6 * share, :LANES]
     turned = vector_all[...].T
     norm = jnp.sqrt(jnp.sum(turned[12:13, :], axis=1, keepdims=True))
@@ -1339,6 +1356,8 @@
         values = adam_update(weight, first, second, grad, factor, rate)
         for part in range(3):
             results[3 * index + part][...] = values[part]
+    for store in stores:
+        store.wait()
 
 
 def fused(devices, features, coords, fourier_basis, block_items, point_mask, cotangent, *weights):
@@ -1447,7 +1466,6 @@
         "sem_out": pltpu.SemaphoreType.DMA((2, 2)),
     }
     for key, rows in (("c", rows_c), ("d", rows_d), ("e", rows_e)):
-        scratch["full_" + key] = vmem((2, 4, outers, rows, width), bf16)
         for part in ("half_", "quarter_"):
             scratch[part + key] = vmem((4, outers, rows, width), bf16)
         scratch["last_" + key] = vmem((outers, rows, width), bf16)
@@ -1471,7 +1489,6 @@
             collective_id=0, has_side_effects=True, vmem_limit_bytes=VMEM_BYTES
         ),
     )(*inputs.values())
-    layer_output, input_grad, *sums = made
     flat = list(weights)
     for part in range(9, 12):
         flat[part] = flat[part].reshape(share, LANES)
@@ -1483,17 +1500,22 @@
         order += [shapes[1 + 3 * index]] * 3
     updated = pl.pallas_call(
         functools.partial(update_kernel, share),
-        out_shape=[shapes[0]] + order,
-        in_specs=[whole] * 22,
-        out_specs=[whole] * 19,
+        out_shape=[jax.ShapeDtypeStruct(*shape) for shape in list(outputs.values())[:2]]
+        + [shapes[0]]
+        + order,
+        in_specs=[pl.BlockSpec(memory_space=pl.ANY)] * 2 + [whole] * 22,
+        out_specs=[pl.BlockSpec(memory_space=pl.ANY)] * 2 + [whole] * 19,
         scratch_shapes=[
             vmem(square.shape, f32),
             vmem(expand.shape, f32),
             vmem(contract.shape, f32),
+            vmem((points, width), bf16),
+            vmem((points, width), f32),
+            pltpu.SemaphoreType.DMA((2, 2, PIECES)),
         ],
-        compiler_params=pltpu.CompilerParams(vmem_limit_bytes=16 * 1024 * 1024),
-    )(*sums, *flat)
-    norm, *rest = updated
+        compiler_params=pltpu.CompilerParams(vmem_limit_bytes=VMEM_BYTES),
+    )(*made, *flat)
+    layer_output, input_grad, norm, *rest = updated
     for part in range(9, 12):
         rest[part] = rest[part].reshape(fourier.shape)
     return (layer_output, input_grad, norm.reshape(()), *rest)

time: 250 us -> 191 us (0.76)
  Pallas kernels: 227 us -> 190 us
  local copies, waits for them, and re-layouts: 21.8 us -> 0 us
    pallas_call x1, Pallas kernels: 226 us -> 183 us  [fused(): pl.pallas_call(functools.partial(layer_kernel, names, devices), out_shape...]
    unnamed x48 -> x0, local copies, waits for them, and re-layouts: 21.8 us -> none
    pallas_call x1, Pallas kernels: 0.97 us -> 7.41 us  [fused(): pl.pallas_call(functools.partial(update_kernel, share), out_shape=[jax.Sh...]
where the time goes in v2:
time: 191 us
  Pallas kernels  190 us (99%)
    pallas_call x1, Pallas kernels, fused(): pl.pallas_call(functools.partial(layer_kernel, names, devices), out_shape...  183 us
    pallas_call x1, Pallas kernels, fused(): pl.pallas_call(functools.partial(update_kernel, share), out_shape=[jax.Sh...  7.41 us

profile of v2, /device:TPU:0, one launch (start us, length us, event | category | flops | bytes accessed | tf_op | source)
XLA Modules:
  0.0 191.3 jit_solution(5734751862253124115)
XLA Ops:
  0.7 183.0 %shard_map.391 = (bf16[4096,256]{1,0:T(8,128)(2,1)}, f32[4096,256]{1,0:T(8,128)}, f32[48,256]{1,0:T(8,128)}, f32[64,256]{1,0:T(8,128)}, f32[32,256]{1,0:T(8,128)}, /*index=5*/f32[256,128]{1,0:T(8,128)}) custom-call(s32[32]{0:T(128)} %refs_0_.1, bf16[4096,256]{1,0:T(8,128)(2,1)} %refs_1_.1, f32[2,4096]{1,0:T(2,128)} %refs_2_.1, f32[2,64]{1,0:T(2,128)} %refs_3_.1, ...), custom_call_target="tpu_custom_call" | custom-call | tf_op jit(solution)/shard_map/pallas_call | solution.py:1482
  183.7 7.4 %shard_map.392 = (bf16[4096,256]{1,0:T(8,128)(2,1)}, f32[4096,256]{1,0:T(8,128)}, f32[1,1]{1,0:T(1,128)}, f32[7,2048]{1,0:T(8,128)}, f32[7,2048]{1,0:T(8,128)}, ...) custom-call(bf16[4096,256]{1,0:T(8,128)(2,1)} %get-tuple-element.48., ...), custom_call_target="tpu_custom_call" | custom-call | tf_op jit(solution)/shard_map/pallas_call | solution.py:1501

commit v3 on v2

--- a/solution.py
+++ b/solution.py
@@ -747,7 +747,7 @@
 def layer_kernel(names, devices, *refs):
     s = types.SimpleNamespace(**dict(zip(names, refs)))
     at = Place(devices)
-    points, width = s.features.shape
+    points, width = s.features_far.shape
     tiles = points // TILE
     blocks = points // BLOCK
     share = width // devices
@@ -765,6 +765,48 @@
             barrier, inc=1, device_id=(at.device(at.outer_at(step), at.inner),),
             device_id_type=pl.DeviceIdType.MESH,
         )
+
+    quarter = points // 4
+    feature_loads = [
+        pltpu.make_async_copy(
+            s.features_far.at[part * quarter : (part + 1) * quarter],
+            s.features.at[part * quarter : (part + 1) * quarter],
+            s.sem_in.at[part],
+        )
+        for part in range(4)
+    ]
+    for load in feature_loads:
+        load.start()
+
+    class Aside:
+        def __init__(self, first, *buffers):
+            self.pairs = []
+            row = first
+            for buffer in buffers:
+                for start in range(0, buffer.shape[0], LANES):
+                    near = buffer.at[start : start + LANES]
+                    far = s.aside.at[row : row + LANES]
+                    self.pairs.append((near, far, s.sem_aside.at[row // LANES]))
+                    row += LANES
+
+        def store(self):
+            for near, far, sem in self.pairs:
+                pltpu.make_async_copy(near, far, sem).start()
+
+        def stored(self):
+            for near, far, sem in self.pairs:
+                pltpu.make_async_copy(near, far, sem).wait()
+
+        def load(self):
+            for near, far, sem in self.pairs:
+                pltpu.make_async_copy(far, near, sem).start()
+
+        def loaded(self):
+            for near, far, sem in self.pairs:
+                pltpu.make_async_copy(far, near, sem).wait()
+
+    aside_a = Aside(0, s.u1, s.kv)
+    aside_b = Aside(3 * width, s.e1, s.o, s.u2, s.u3)
 
     def columns(tile):
         return pl.ds(pl.multiple_of(tile * TILE, TILE), TILE)
@@ -835,7 +877,6 @@
     one = Gather(at, s.gather_one, (s.sem_g1s, s.sem_g1r))
     two = Gather(at, s.gather_two, (s.sem_g2s, s.sem_g2r))
     one.start_first()
-    two.start_first()
 
     row_at = lax.broadcasted_iota(jnp.int32, (width, width), 0)
     lane_at = lax.broadcasted_iota(jnp.int32, (width, width), 1)
@@ -856,8 +897,6 @@
         (item_wide == rows_wide // E) & (rows_wide % E == lanes_wide % E), 1.0, 0.0
     ).astype(jnp.bfloat16)
     s.vector_sum[...] = jnp.zeros(s.vector_sum.shape, f32)
-    for grad in (s.grad_qkv, s.grad_o, s.grad_kv, s.grad_do, s.grad_w1, s.grad_p1, s.grad_w2, s.grad_p2, s.grad_dq):
-        grad[...] = jnp.zeros(grad.shape, f32)
     speed = (lax.broadcasted_iota(jnp.int32, (E // 4, 1), 0).astype(f32) + 1.0) * (
         math.pi / (E // 4)
     )
@@ -886,8 +925,11 @@
                 s.point_mask[pl.ds(tile * tile_blocks + block, 1), :].astype(f32)
             )
 
+    for load in feature_loads:
+        load.wait()
     lax.fori_loop(0, tiles // 4, before, None)
     one.start_second()
+    two.start_first()
     lax.fori_loop(tiles // 4, tiles // 2, before, None)
     one.start_third()
     two.start_second()
@@ -957,14 +999,15 @@
         s.q[:, where] = low(turn(projected[:width], cosine, sine, 1.0))
         keys = low(turn(projected[width : 2 * width], cosine, sine, 1.0) * s.mask[0:1, where])
         values = low(projected[2 * width :])
-        s.k[:, where] = keys
-        s.v[:, where] = values
+        s.kv[:width, where] = keys
+        s.kv[width:, where] = values
         put_products(tile, values, keys)
 
-    lax.fori_loop(0, tiles // 2, phase_a, None)
+    lax.fori_loop(0, tiles, phase_a, None)
+    table_sum = TableSum(at, s)
+    table_sum.start()
+    aside_a.store()
     two.start_third()
-    lax.fori_loop(tiles // 2, tiles, phase_a, None)
-    two.finish()
 
     def take_two(index, carried):
         parts = chunk_pair(s.gather_two, index)
@@ -993,8 +1036,8 @@
         )
         return tuple(found)
 
-    table_sum = TableSum(at, s)
-    table_sum.start()
+    table_sum.middle()
+    two.finish()
     found = lax.fori_loop(
         0, devices // group, take_two, tuple(jnp.zeros((1, LANES), f32) for _ in range(at.outers))
     )
@@ -1005,8 +1048,8 @@
     w_dq = jnp.concatenate(
         [s.fourier[pl.ds(0, FOUR, stride=2), :], s.fourier[pl.ds(1, FOUR, stride=2), :]], axis=1
     )
-    table_sum.middle()
     s.t_dq[...] = low(w_dq.T)
+    table_sum.late(s.table_self)
     for piece in range(2):
         cols = slice(piece * width, (piece + 1) * width)
         s.t_kv[cols, :] = flip(s.w_kv[:, cols])
@@ -1015,13 +1058,6 @@
         s.t_w2[:, cols] = flip(s.w_w2[cols, :])
         s.t_p2[:, cols] = flip(s.w_p2[cols, :])
     s.t_do[...] = flip(s.w_do[...])
-    table_sum.late(s.table_self)
-
-    def cross_queries(tile, _):
-        where = columns(tile)
-        s.qd[:, where] = low(dot(s.t_dq[...], s.phi[:, where]))
-
-    lax.fori_loop(0, tiles, cross_queries, None)
     table_sum.finish(s.table_self)
 
     def phase_b(tile, _):
@@ -1039,10 +1075,10 @@
         s.xh2[:, where] = low(scaled_two)
         middle = low(scaled_two * column(2) + column(3))
         s.u2[:, where] = middle
-        hidden, slope = gelu_both(dot(s.t_w1[...], middle) + hidden_column(0))
-        hidden = low(hidden)
+        hidden_pre = dot(s.t_w1[...], middle) + hidden_column(0)
+        hidden = low(gelu(hidden_pre))
         s.e1[:, where] = hidden
-        s.slope[:, where] = low(slope)
+        s.slope[:, where] = low(hidden_pre)
         encoded = first_sum + dot(s.t_w2[...], hidden) + column(6)
         scaled_three, root_three = column_norm(encoded)
         s.root_three[0:1, where] = root_three
@@ -1052,14 +1088,48 @@
         pair = dot(s.t_kv[...], outer)
         keys = low(pair[:width] * mask)
         values = low(pair[width:])
-        s.kd[:, where] = keys
-        s.vd[:, where] = values
+        s.kvd[:width, where] = keys
+        s.kvd[width:, where] = values
         put_products(tile, values, keys)
 
     lax.fori_loop(0, tiles, phase_b, None)
     table_sum.start()
+    aside_b.store()
+
+    def cotangent_load(tile):
+        slot = lax.rem(tile, 2)
+        where = pl.ds(pl.multiple_of(tile * TILE, TILE), TILE)
+        return pltpu.make_async_copy(
+            s.cotangent_far.at[where, :], s.output_slots.at[slot], s.sem_in.at[4 + slot]
+        )
+
+    cotangent_load(0).start()
+    cotangent_load(1).start()
+    aside_a.stored()
+
+    def cross_inputs(tile, _):
+        where = columns(tile)
+        s.qd[:, where] = low(dot(s.t_dq[...], s.phi[:, where]))
+        cotangent_load(tile).wait()
+        upstream = s.output_slots[lax.rem(tile, 2)]
+        turned = upstream.T
+        s.u1[:, where] = turned
+        add_sum(7, turned.astype(f32))
+        s.kv[:, where] = low(dot(s.w_p2[...], turned))
+
+        @pl.when(tile + 2 < tiles)
+        def _():
+            cotangent_load(tile + 2).start()
+
+    def slopes(tile, _):
+        where = columns(tile)
+        s.slope[:, where] = low(gelu_slope(s.slope[:, where].astype(f32)))
+
+    lax.fori_loop(0, tiles, cross_inputs, None)
     table_sum.middle()
+    lax.fori_loop(0, tiles, slopes, None)
     table_sum.late(s.table_other)
+    aside_b.stored()
     table_sum.finish(s.table_other)
 
     def phase_c(tile, _):
@@ -1070,34 +1140,45 @@
         decoded = low(
             per_block(tile, lambda b: dot(tables[b], queries[:, lanes_of(b)])) * mask
         )
-        latent = dot(s.t_do[...], decoded)
-        latent_low = low(latent)
+        s.u2[:, where] = decoded
+        latent_low = low(dot(s.t_do[...], decoded))
+        s.o[:, where] = latent_low
         hidden, slope = gelu_both(dot(s.t_p1[...], latent_low) + hidden_column(1))
-        hidden = low(hidden)
-        output = latent + dot(s.t_p2[...], hidden) + column(7)
-        put_out(tile, s.layer_output, s.output_slots, s.sem_out, 0, low(output).T)
-        upstream = s.cotangent[where, :]
-        turned = dot_bt(s.eye[...], upstream)
-        add_sum(7, turned)
-        grad_spread = dot_bt(s.w_p2[...], upstream) * slope
+        s.e1[:, where] = low(hidden)
+        grad_spread = s.kv[:, where].astype(f32) * slope
         add_sum(10, grad_spread)
         grad_spread = low(grad_spread)
-        grad_latent = low(turned + dot(s.w_p1[...], grad_spread))
+        s.kv[:, where] = grad_spread
+        grad_latent = low(s.u1[:, where].astype(f32) + dot(s.w_p1[...], grad_spread))
+        s.u3[:, where] = grad_latent
         grad_decoded = low(dot(s.w_do[...], grad_latent) * mask)
-        grad_queries = low(
-            per_block(tile, lambda b: dot_at(tables[b], grad_decoded[:, lanes_of(b)]))
-        )
         put_products(tile, grad_decoded, queries)
-        s.grad_p2[...] += dot(hidden, upstream)
-        s.grad_p1[...] += dot_bt(latent_low, grad_spread)
-        s.grad_do[...] += dot_bt(decoded, grad_latent)
-        s.grad_dq[...] += dot_bt(s.phi[:, where], grad_queries)
+        s.qd[:, where] = grad_decoded
 
     lax.fori_loop(0, tiles, phase_c, None)
     table_sum.start()
-    end_out(s.layer_output, s.output_slots, s.sem_out, 0)
+
+    def cross_query_grads(tile, _):
+        where = columns(tile)
+        upstream = s.qd[:, where]
+        grad = per_block(
+            tile, lambda b: dot_at(summary(s.table_other, tile, b), upstream[:, lanes_of(b)])
+        )
+        s.qd[:, where] = low(grad)
+
+    def outputs(tile, _):
+        where = columns(tile)
+        output = dot(s.t_do[...], s.u2[:, where]) + dot(s.t_p2[...], s.e1[:, where]) + column(7)
+        put_out(tile, s.layer_output, s.output_slots, s.sem_out, 0, low(output).T)
+
+    lax.fori_loop(0, tiles, cross_query_grads, None)
+    s.grad_dq[...] = dot_bt(s.phi[...], s.qd[...])
     s.fourier[pl.ds(0, FOUR, stride=2), :] = s.grad_dq[:, :LANES]
     s.fourier[pl.ds(1, FOUR, stride=2), :] = s.grad_dq[:, LANES:]
+    s.grad_do[...] = dot_bt(s.u2[...], s.u3[...])
+    table_sum.middle()
+    s.grad_p1[...] = dot_bt(s.o[...], s.kv[...])
+    s.grad_p2[...] = dot_bt(s.e1[...], s.u1[...])
     zeros = jnp.zeros((share, LANES), f32)
 
     def rows_of(chunk, count=1):
@@ -1119,20 +1200,23 @@
 
     sum_c = GradSum(at, s, "c", 0)
     sum_c.start(chunk_c)
-    table_sum.middle()
+    table_sum.late(s.table_third)
+    lax.fori_loop(0, tiles, outputs, None)
+    end_out(s.layer_output, s.output_slots, s.sem_out, 0)
+    aside_a.load()
+    aside_b.load()
     sum_c.second()
-    table_sum.late(s.table_other)
-    table_sum.finish(s.table_other)
+    table_sum.finish(s.table_third)
 
     def phase_d(tile, _):
         where = columns(tile)
         mask = s.mask[0:1, where]
-        keys, values = s.kd[:, where], s.vd[:, where]
-        tables = [summary(s.table_other, tile, block) for block in range(tile_blocks)]
+        keys, values = s.kvd[:width, where], s.kvd[width:, where]
+        tables = [summary(s.table_third, tile, block) for block in range(tile_blocks)]
         grad_keys = per_block(tile, lambda b: dot_at(tables[b], values[:, lanes_of(b)])) * mask
         grad_values = per_block(tile, lambda b: dot(tables[b], keys[:, lanes_of(b)]))
         grad_pair = low(jnp.concatenate([grad_keys, grad_values], axis=0))
-        s.grad_kv[...] += dot_bt(s.u3[:, where], grad_pair)
+        s.kvd[:, where] = grad_pair
         grad_outer = dot(s.w_kv[...], grad_pair)
         scaled = s.xh3[:, where].astype(f32)
         add_sum(4, grad_outer * scaled)
@@ -1142,11 +1226,11 @@
         )
         add_sum(6, grad_encoded)
         grad_encoded_low = low(grad_encoded)
-        s.grad_w2[...] += dot_bt(s.e1[:, where], grad_encoded_low)
+        s.xh3[:, where] = grad_encoded_low
         grad_hidden = dot(s.w_w2[...], grad_encoded_low) * s.slope[:, where].astype(f32)
         add_sum(8, grad_hidden)
         grad_hidden = low(grad_hidden)
-        s.grad_w1[...] += dot_bt(s.u2[:, where], grad_hidden)
+        s.slope[:, where] = grad_hidden
         grad_middle = dot(s.w_w1[...], grad_hidden)
         scaled = s.xh2[:, where].astype(f32)
         add_sum(2, grad_middle * scaled)
@@ -1156,9 +1240,8 @@
         )
         grad_first = low(grad_first)
         s.xh2[:, where] = grad_first
-        s.grad_o[...] += dot_bt(s.o[:, where], grad_first)
         grad_attended = low(dot(s.w_o[...], grad_first) * mask)
-        s.kd[:, where] = grad_attended
+        s.qd[:, where] = grad_attended
         put_products(tile, grad_attended, s.q[:, where])
 
     lax.fori_loop(0, tiles // 2, phase_d, None)
@@ -1166,6 +1249,24 @@
     lax.fori_loop(tiles // 2, tiles, phase_d, None)
     table_sum.start()
     s.grads_c[...] = sum_c.finish()
+    aside_a.loaded()
+    aside_b.loaded()
+
+    def query_grads(tile, _):
+        where = columns(tile)
+        upstream = s.qd[:, where]
+        grad = per_block(
+            tile, lambda b: dot_at(summary(s.table_self, tile, b), upstream[:, lanes_of(b)])
+        )
+        s.q[:, where] = low(turn(grad, s.cosine[:, where], s.sine[:, where], -1.0))
+
+    lax.fori_loop(0, tiles, query_grads, None)
+    s.grad_o[...] = dot_bt(s.o[...], s.xh2[...])
+    table_sum.middle()
+    s.grad_kv[...] = dot_bt(s.u3[...], s.kvd[...])
+    s.grad_w2[...] = dot_bt(s.e1[...], s.xh3[...])
+    s.grad_w1[...] = dot_bt(s.u2[...], s.slope[...])
+    table_sum.late(s.table_other)
 
     def chunk_d(chunk):
         where = rows_of(chunk)
@@ -1184,35 +1285,43 @@
 
     sum_d = GradSum(at, s, "d", 0)
     sum_d.start(chunk_d)
-    table_sum.middle()
-
-    def query_grads(tile, _):
-        where = columns(tile)
-        upstream = s.kd[:, where]
-        grad = per_block(
-            tile, lambda b: dot_at(summary(s.table_self, tile, b), upstream[:, lanes_of(b)])
-        )
-        grad = low(turn(grad, s.cosine[:, where], s.sine[:, where], -1.0))
-        s.q[:, where] = grad
-        s.grad_qkv[:, :width] += dot_bt(s.u1[:, where], grad)
-
-    lax.fori_loop(0, tiles // 2, query_grads, None)
-    sum_d.second()
-    table_sum.late(s.table_other)
-    lax.fori_loop(tiles // 2, tiles, query_grads, None)
+    s.grad_qkv[:, :width] = dot_bt(s.u1[...], s.q[...])
     table_sum.finish(s.table_other)
 
     def phase_e(tile, _):
         where = columns(tile)
         mask = s.mask[0:1, where]
-        keys, values = s.k[:, where], s.v[:, where]
+        keys, values = s.kv[:width, where], s.kv[width:, where]
         tables = [summary(s.table_other, tile, block) for block in range(tile_blocks)]
         grad_keys = per_block(tile, lambda b: dot_at(tables[b], values[:, lanes_of(b)])) * mask
         grad_values = low(per_block(tile, lambda b: dot(tables[b], keys[:, lanes_of(b)])))
-        grad_keys = low(turn(grad_keys, s.cosine[:, where], s.sine[:, where], -1.0))
-        pair = jnp.concatenate([grad_keys, grad_values], axis=0)
-        s.grad_qkv[:, width:] += dot_bt(s.u1[:, where], pair)
-        grad_normed = dot(s.w_qkv[...], jnp.concatenate([s.q[:, where], pair], axis=0))
+        s.kv[:width, where] = low(turn(grad_keys, s.cosine[:, where], s.sine[:, where], -1.0))
+        s.kv[width:, where] = grad_values
+
+    lax.fori_loop(0, tiles, phase_e, None)
+    sum_d.second()
+    s.grad_qkv[:, width:] = dot_bt(s.u1[...], s.kv[...])
+
+    def chunk_e(chunk):
+        where = rows_of(chunk)
+        return jnp.concatenate(
+            [
+                s.grad_qkv[where, :width],
+                s.grad_qkv[where, width : 2 * width],
+                s.grad_qkv[where, 2 * width :],
+                jnp.zeros((share, width), f32),
+            ],
+            axis=0,
+        )
+
+    sum_e = GradSum(at, s, "e", 8 * share)
+    sum_e.start(chunk_e)
+
+    def phase_f(tile, _):
+        where = columns(tile)
+        grad_normed = dot(
+            s.w_qkv[...], jnp.concatenate([s.q[:, where], s.kv[:, where]], axis=0)
+        )
         turned = features_turned(tile)
         root = s.root_one[0:1, where]
         scaled = (turned - jnp.sum(turned, axis=0, keepdims=True) * (1.0 / width)) * root
@@ -1223,9 +1332,20 @@
         )
         put_out(tile, s.input_grad, s.input_slots, s.sem_out, 1, grad_input.T)
 
-    lax.fori_loop(0, tiles // 2, phase_e, None)
+    lax.fori_loop(0, tiles // 4, phase_f, None)
+    sum_e.second()
+    lax.fori_loop(tiles // 4, tiles // 2, phase_f, None)
     sum_d.third()
-    lax.fori_loop(tiles // 2, tiles, phase_e, None)
+    lax.fori_loop(tiles // 2, 3 * tiles // 4, phase_f, None)
+    sum_e.third()
+    lax.fori_loop(3 * tiles // 4, tiles, phase_f, None)
+    end_out(s.input_grad, s.input_slots, s.sem_out, 1)
+    s.grads_d[...] = sum_d.finish()
+    s.grads_e[...] = sum_e.finish()
+    squares = sum(
+        jnp.sum(grads[...] * grads[...], axis=0, keepdims=True)
+        for grads in (s.grads_c, s.grads_d, s.grads_e)
+    )
 
     lane_wide = lax.broadcasted_iota(jnp.int32, (width, LANES), 1)
     sums = jnp.zeros((width, LANES), f32)
@@ -1234,64 +1354,41 @@
             lane_wide == index, jnp.sum(s.vector_sum[index], axis=1, keepdims=True), sums
         )
     s.vector_cols[...] = sums
-
-    def chunk_e(chunk):
-        where = rows_of(chunk)
-        return jnp.concatenate(
-            [
-                s.grad_qkv[where, :width],
-                s.grad_qkv[where, width : 2 * width],
-                s.grad_qkv[where, 2 * width :],
-                jnp.concatenate([s.vector_cols[where, :], zeros], axis=1),
-            ],
-            axis=0,
-        )
-
-    sum_e = GradSum(at, s, "e", 8 * share)
-    sum_e.start(chunk_e)
-    s.grads_d[...] = sum_d.finish()
-    end_out(s.input_grad, s.input_slots, s.sem_out, 1)
-    sum_e.second()
-    early = jnp.sum(s.grads_c[...] * s.grads_c[...], axis=0, keepdims=True) + jnp.sum(
-        s.grads_d[...] * s.grads_d[...], axis=0, keepdims=True
-    )
-    sum_e.third()
-    grads_e = sum_e.finish()
-    s.grads_e[...] = grads_e
-    squares = jnp.sum(early + jnp.sum(grads_e * grads_e, axis=0, keepdims=True), axis=1, keepdims=True)
-    vector_rows = grads_e[3 * share : 4 * share, :LANES]
-    row_small = lax.broadcasted_iota(jnp.int32, (share, LANES), 0)
-    lane_small = lax.broadcasted_iota(jnp.int32, (share, LANES), 1)
-    s.final[at.inner, at.outer] = jnp.where(
-        (row_small == 0) & (lane_small == 12), squares, vector_rows
-    )
-
-    def final_along(step, start):
+    turned_sums = s.vector_cols[...].T
+    s.final_inner[at.inner] = jnp.concatenate(
+        [turned_sums[:12], squares, jnp.zeros((3, width), f32)], axis=0
+    )
+
+    def final_near(step, start):
+        source = at.inner if start else at.inner_at(step)
+        return remote(
+            s.final_inner.at[at.inner], s.final_inner.at[source], s.sem_fs.at[0, step],
+            s.sem_fr.at[0, source], at.device(at.outer, at.inner_at(step)),
+        )
+
+    def final_far(step, start):
         source = at.outer if start else at.outer_at(step)
         return remote(
-            s.final.at[at.inner, at.outer], s.final.at[at.inner, source], s.sem_fs.at[0, step],
-            s.sem_fr.at[0, source], at.device(at.outer_at(step), at.inner),
-        )
-
-    def final_inner(step, start):
-        source = at.inner if start else at.inner_at(step)
-        return remote(
-            s.final.at[at.inner], s.final.at[source], s.sem_fs.at[1, step],
-            s.sem_fr.at[1, source], at.device(at.outer, at.inner_at(step)),
-        )
-
+            s.final_outer.at[at.outer], s.final_outer.at[source], s.sem_fs.at[1, step],
+            s.sem_fr.at[1, source], at.device(at.outer_at(step), at.inner),
+        )
+
+    for step in range(1, GROUP):
+        final_near(step, True).start()
+    for step in range(1, GROUP):
+        final_near(step, False).wait()
+    total = s.final_inner[0]
+    for index in range(1, GROUP):
+        total = total + s.final_inner[index]
+    s.final_outer[at.outer] = total
     for step in range(1, at.outers):
-        final_along(step, True).start()
+        final_far(step, True).start()
     for step in range(1, at.outers):
-        final_along(step, False).wait()
-    for step in range(1, GROUP):
-        final_inner(step, True).start()
-    for step in range(1, GROUP):
-        final_inner(step, False).wait()
-
-    @pl.loop(0, devices)
-    def _(chunk):
-        s.vector_all[rows_of(chunk), :] = s.final[lax.rem(chunk, GROUP), lax.div(chunk, GROUP)]
+        final_far(step, False).wait()
+    total = s.final_outer[0]
+    for index in range(1, at.outers):
+        total = total + s.final_outer[index]
+    s.vector_all[...] = total
 
 
 def update_kernel(share, *refs):
@@ -1338,8 +1435,9 @@
         load.wait()
         store.start()
     fourier = grads_c[5 * share : 6 * share, :LANES]
-    turned = vector_all[...].T
-    norm = jnp.sqrt(jnp.sum(turned[12:13, :], axis=1, keepdims=True))
+    turned = vector_all[...]
+    rows = jnp.sum(turned[:12] * turned[:12], axis=0, keepdims=True) + turned[12:13]
+    norm = jnp.sqrt(jnp.sum(rows, axis=1, keepdims=True))
     norm_out[...] = norm
     factor = jnp.minimum(1.0, CLIP_NORM / (norm + 1e-06))
     hidden = jnp.concatenate(
@@ -1371,11 +1469,11 @@
     vmem = lambda shape, dtype: pltpu.VMEM(shape, dtype)
     inputs = {
         "items": block_items,
-        "features": features,
+        "features_far": features,
         "coords": coords,
         "fourier_basis": fourier_basis,
         "point_mask": point_mask.reshape(blocks, BLOCK),
-        "cotangent": cotangent,
+        "cotangent_far": cotangent,
         "square_weight": square,
         "expand_weight": expand,
         "contract_weight": contract,
@@ -1390,7 +1488,8 @@
         "grads_c": ((rows_c, width), f32),
         "grads_d": ((rows_d, width), f32),
         "grads_e": ((rows_e, width), f32),
-        "vector_all": ((width, LANES), f32),
+        "vector_all": ((16, width), f32),
+        "aside": ((8 * width, points), bf16),
     }
     tall = lambda rows: vmem((rows, points), bf16)
     scratch = {
@@ -1440,8 +1539,7 @@
         "phi": tall(FOUR),
         "u1": tall(width),
         "q": tall(width),
-        "k": tall(width),
-        "v": tall(width),
+        "kv": tall(2 * width),
         "qd": tall(width),
         "o": tall(width),
         "xh2": tall(width),
@@ -1450,8 +1548,7 @@
         "slope": tall(F),
         "xh3": tall(width),
         "u3": tall(width),
-        "kd": tall(width),
-        "vd": tall(width),
+        "kvd": tall(2 * width),
         "per_block": vmem((blocks * E, width), f32),
         "inverse": vmem((max(8, outers), width), f32),
         "table_send": vmem((GROUP, outers, 16, width), bf16),
@@ -1460,7 +1557,12 @@
         "table_cross": vmem((2, outers, outers, 16, width), bf16),
         "table_self": vmem((GROUP, outers, 16, width), bf16),
         "table_other": vmem((GROUP, outers, 16, width), bf16),
-        "final": vmem((GROUP, outers, share, LANES), f32),
+        "final_inner": vmem((GROUP, 16, width), f32),
+        "final_outer": vmem((outers, 16, width), f32),
+        "features": vmem((points, width), bf16),
+        "sem_in": pltpu.SemaphoreType.DMA((6,)),
+        "sem_aside": pltpu.SemaphoreType.DMA((8 * width // LANES,)),
+        "table_third": vmem((GROUP, outers, 16, width), bf16),
         "output_slots": vmem((2, TILE, width), bf16),
         "input_slots": vmem((2, TILE, width), f32),
         "sem_out": pltpu.SemaphoreType.DMA((2, 2)),
@@ -1475,15 +1577,16 @@
     for key in ("fs", "fr"):
         scratch["sem_" + key] = pltpu.SemaphoreType.DMA((2, many))
     names = list(inputs) + list(outputs) + list(scratch)
-    in_specs = [pl.BlockSpec(memory_space=pltpu.SMEM)] + [
-        pl.BlockSpec(memory_space=pltpu.VMEM) for _ in range(len(inputs) - 1)
-    ]
+    spaces = {"items": pltpu.SMEM, "features_far": pl.ANY, "cotangent_far": pl.ANY}
+    in_specs = [pl.BlockSpec(memory_space=spaces.get(name, pltpu.VMEM)) for name in inputs]
     whole = pl.BlockSpec(memory_space=pltpu.VMEM)
     made = pl.pallas_call(
         functools.partial(layer_kernel, names, devices),
         out_shape=[jax.ShapeDtypeStruct(*shape) for shape in outputs.values()],
         in_specs=in_specs,
-        out_specs=[pl.BlockSpec(memory_space=pl.ANY)] * 2 + [whole] * (len(outputs) - 2),
+        out_specs=[pl.BlockSpec(memory_space=pl.ANY)] * 2
+        + [whole] * 4
+        + [pl.BlockSpec(memory_space=pl.ANY)],
         scratch_shapes=list(scratch.values()),
         compiler_params=pltpu.CompilerParams(
             collective_id=0, has_side_effects=True, vmem_limit_bytes=VMEM_BYTES
@@ -1514,7 +1617,7 @@
             pltpu.SemaphoreType.DMA((2, 2, PIECES)),
         ],
         compiler_params=pltpu.CompilerParams(vmem_limit_bytes=VMEM_BYTES),
-    )(*made, *flat)
+    )(*made[:6], *flat)
     layer_output, input_grad, norm, *rest = updated
     for part in range(9, 12):
         rest[part] = rest[part].reshape(fourier.shape)

time: 191 us -> 167 us (0.87)
  Pallas kernels: 190 us -> 166 us
    pallas_call x1, Pallas kernels: 183 us -> 159 us  [fused(): pl.pallas_call(functools.partial(layer_kernel, names, devices), out_shape...]
where the time goes in v3:
time: 167 us
  Pallas kernels  166 us (99%)
    pallas_call x1, Pallas kernels, fused(): pl.pallas_call(functools.partial(layer_kernel, names, devices), out_shape...  159 us
    pallas_call x1, Pallas kernels, fused(): pl.pallas_call(functools.partial(update_kernel, share), out_shape=[jax.Sh...  7.36 us

profile of v3, /device:TPU:0, one launch (start us, length us, event | category | flops | bytes accessed | tf_op | source)
XLA Modules:
  0.0 166.9 jit_solution(9937118414910510636)
XLA Ops:
  0.7 158.7 %shard_map.391 = (bf16[4096,256]{1,0:T(8,128)(2,1)}, f32[4096,256]{1,0:T(8,128)}, f32[48,256]{1,0:T(8,128)}, f32[64,256]{1,0:T(8,128)}, f32[32,256]{1,0:T(8,128)...) custom-call(s32[32]{0:T(128)} %refs_0_.1, bf16[4096,256]{1,0:T(8,128)(2,1)} %refs_1_.1, f32[2,4096]{1,0:T(2,128)} %refs_2_.1, ...), custom_call_target="tpu_custom_call" | custom-call | tf_op jit(solution)/shard_map/pallas_call | solution.py:1583
  159.4 7.4 %shard_map.392 = (bf16[4096,256]{1,0:T(8,128)(2,1)}, f32[4096,256]{1,0:T(8,128)}, f32[1,1]{1,0:T(1,128)}, f32[7,2048]{1,0:T(8,128)}, f32[7,2048]{1,0:T(8,128)}, ...) custom-call(bf16[4096,256]{1,0:T(8,128)(2,1)} %get-tuple-element.48., ...), custom_call_target="tpu_custom_call" | custom-call | tf_op jit(solution)/shard_map/pallas_call | solution.py:1604
